TPU v7x, 256 devices: a whole 4x4x8 slice. The times are simulated.
256 devices in a mesh: rep: 8 (over y, core), wide: 32 (over z, x).
Axes of the slice: x: 4, y: 4, z: 8, core: 2. Of those that a mesh axis runs over, the one named last changes fastest.
Arguments:
- shard_lost: int32 [8], replicated, may hold values from 0 to 31, as said below
- new_blocks: int32 [28], replicated, may hold values from 1 to 3, as said below
- weights: float32 [8, 4096, 1536], P('rep', 'wide'), may hold values from -3 to 3, as said below
- first_moment: float32 [8, 4096, 1536], P('rep', 'wide'), may hold values from -2 to 2, as said below
- second_moment: float32 [8, 4096, 1536], P('rep', 'wide'), may hold values from 0.05 to 1, as said below
- gradient: bfloat16 [8, 4096, 1536], P('rep', 'wide'), may hold values from -1200 to 1200
Outputs:
- new_weights: float32 [8, 12288, 1536], P('rep', 'wide')
- new_first: float32 [8, 12288, 1536], P('rep', 'wide')
- new_second: float32 [8, 12288, 1536], P('rep', 'wide')
Inputs may be any that keep to these rules, and one draw needn't show every extreme that they name: `shard_lost`: the 8 values are distinct; one island lost shard 0 and another lost the last shard. `new_blocks`: the counts sum to 32; exactly one of them equals 3. All islands hold the same weights, except the 128 rows that each island lost at its lost shard, which hold arbitrary values. `first_moment`: same for the first moments. `second_moment`: same for the second moments.
All inputs are finite; a program needn't handle non-finite values.
Results may differ from a plain program's by a relative error of at most 0.0003.
Values may be sent and summed in bfloat16 or wider, within the bound.
A program may use at most 64 MiB of HBM per device.

v0:
```python
import math

import jax
import jax.numpy as jnp
from jax import lax
from jax.sharding import PartitionSpec as P

beta_first = 0.9
beta_second = 0.95
bias_first = 1.0 - 0.9**20
bias_second = 1.0 - 0.95**20
learn_rate = 0.01
weight_decay = 0.1
eps_adam = 1e-08


def shifted(value, axis, steps):
    count = lax.axis_size(axis)
    initial, last = (max(0, -steps), min(count, count - steps))
    return lax.ppermute(value, axis, [(source, source + steps) for source in range(initial, last)])


def passed_along(value, axis, steps):
    count = lax.axis_size(axis)
    pairs = [(source, (source + steps) % count) for source in range(count)]
    return lax.ppermute(value, axis, pairs)


def adam_update(params, moment_one, moment_two, grad_in, factor):
    clipped = grad_in.astype(jnp.float32) * factor
    one_new = beta_first * moment_one + (1.0 - beta_first) * clipped
    two_new = beta_second * moment_two + (1.0 - beta_second) * clipped * clipped
    step_dir = one_new / bias_first / (jnp.sqrt(two_new / bias_second) + eps_adam)
    params_new = params - learn_rate * (step_dir + weight_decay * params)
    return (params_new, one_new, two_new)


def neighbours(stacked, max_shift):
    pieces = [stacked]
    for distance in range(1, max_shift + 1):
        pieces.append(shifted(stacked, "wide", -distance))
    return jnp.stack(pieces)


def grad_neighbours(grad_in, max_shift):
    pieces = [grad_in]
    for distance in range(1, max_shift + 1):
        pieces.append(shifted(grad_in, "wide", -distance))
    return jnp.stack(pieces)


def on_device(shard_lost, new_blocks, weights, first_moment, second_moment, gradient):
    shards = lax.axis_size("wide")
    islands = lax.axis_size("rep")
    max_shift = shards // 8
    cap_blocks = 1 + min(2, max_shift)
    block_rows = weights.shape[1]
    island = lax.axis_index("rep")
    shard_index = lax.axis_index("wide")
    stacked = jnp.stack([weights, first_moment, second_moment])
    peer_copy = passed_along(stacked, "rep", -1)
    is_island = jnp.arange(islands, dtype=jnp.int32) == island
    my_lost = jnp.sum(jnp.where(is_island, shard_lost, 0))
    broken = shard_index == my_lost
    stacked = jnp.where(broken, peer_copy, stacked)
    local_sum = jnp.sum(jnp.square(gradient.astype(jnp.float32)))
    norm_sum = lax.psum(local_sum, "wide")
    limit = 0.5 * math.sqrt(block_rows * shards * gradient.shape[2])
    factor = jnp.minimum(1.0, limit / (jnp.sqrt(norm_sum) + 1e-06))
    counts = jnp.concatenate([new_blocks, jnp.zeros((max_shift,), jnp.int32)])
    starts = jnp.cumsum(counts) - counts
    is_mine = jnp.arange(shards, dtype=jnp.int32) == shard_index
    first_block = jnp.sum(jnp.where(is_mine, starts, 0))
    block_count = jnp.sum(jnp.where(is_mine, counts, 0))
    blocks = []
    window = neighbours(stacked, max_shift)
    grad_window = grad_neighbours(gradient, max_shift)
    for offset in range(cap_blocks):
        source_gap = jnp.clip(first_block + offset - shard_index, 0, max_shift)
        picked = lax.dynamic_index_in_dim(window, source_gap, 0, keepdims=False)
        picked_grad = lax.dynamic_index_in_dim(grad_window, source_gap, 0, keepdims=False)
        updated = jnp.stack(adam_update(picked[0], picked[1], picked[2], picked_grad, factor))
        blocks.append(jnp.where(offset < block_count, updated, 0.0))
    result = jnp.concatenate(blocks, axis=2)
    return (result[0], result[1], result[2])


def solution(mesh):
    return jax.shard_map(
        on_device,
        mesh=mesh,
        in_specs=(
            P(),
            P(),
            P("rep", "wide", None),
            P("rep", "wide", None),
            P("rep", "wide", None),
            P("rep", "wide", None),
        ),
        out_specs=(P("rep", "wide", None), P("rep", "wide", None), P("rep", "wide", None)),
        check_vma=False,
    )
```

profile of v0, /device:TPU:176, one launch (start us, length us, event | category | flops | bytes accessed | tf_op | source)
XLA Modules:
  0.0 397.6 jit_solution(7327356163474340109)
XLA Ops:
  0.7 3.3 pad_maximum_fusion.1
  4.0 5.1 %collective-permute-start.5 = (bf16[1,128,1536]{2,1,0:T(8,128)(2,1)S(1)}, bf16[1,128,1536]{2,1,0:T(8,128)(2,1)}, u32[]{:S(2)}, u32[]{:S(2)}) collective-permute-start(bf16[1,128,1536]{2,1,0:T(8,128)(2,1)S(1)} %copy-done.3), channel_id=1, source_target_pairs={{1,0},{2,1},{3,2},{4,3},{5,4},{6,5},{7,6},{8,7},{9,8},{10,9},{11,1... | collective-permute-start | bytes 1179656 | tf_op jit(solution)/shard_map/ppermute | solution.py:20
  9.1 2.7 collective-permute-start.6
  11.8 2.3 collective-permute-start.7
  14.2 0.8 multiply_reduce_fusion
  15.0 2.0 collective-permute-start.8
  17.0 94.5 %psum.7 = f32[]{:T(128)} all-reduce(f32[]{:T(128)} %multiply_reduce_fusion), channel_id=1, replica_groups=mesh['rep'=8,'wide'=32] {'wide'}, use_global_device_ids=true, to_apply=%region_5.6 | all-reduce | flops 1 | bytes 8 | tf_op jit(solution)/shard_map/psum | solution.py:67
  112.0 0.7 copy.18
  113.4 0.8 reduce
  114.2 1.3 fusion.12
  119.4 1.3 fusion.14
  122.6 1.9 collective-permute-start.1
  124.6 6.3 %collective-permute-start.2 = (f32[3,1,128,1536]{3,2,0,1:T(8,128)S(1)}, f32[3,1,128,1536]{3,2,0,1:T(8,128)S(1)}, u32[]{:S(2)}, u32[]{:S(2)}) collective-permute-start(f32[3,1,128,1536]{3,2,0,1:T(8,128)S(1)} %get-tuple-element.15), channel_id=1, source_target_pairs={{2,0},{3,1},{4,2},{5,3},{6,4},{7,5},{8,6},{9,7},{10,8},{11,9},{12,... | collective-permute-start | bytes 7077896 | tf_op jit(solution)/shard_map/ppermute | solution.py:20
  130.9 1.0 bitcast_dynamic-update-slice_fusion.8
  131.9 5.2 %collective-permute-start.3 = (f32[3,1,128,1536]{3,2,0,1:T(8,128)S(1)}, f32[3,1,128,1536]{3,2,0,1:T(8,128)S(1)}, u32[]{:S(2)}, u32[]{:S(2)}) collective-permute-start(f32[3,1,128,1536]{3,2,0,1:T(8,128)S(1)} %get-tuple-element.15), channel_id=1, source_target_pairs={{3,0},{4,1},{5,2},{6,3},{7,4},{8,5},{9,6},{10,7},{11,8},{12,9},{13... | collective-permute-start | bytes 7077896 | tf_op jit(solution)/shard_map/ppermute | solution.py:20
  137.1 1.0 bitcast_dynamic-update-slice_fusion.7
  138.2 1.9 collective-permute-start.4
  140.2 74.3 %collective-permute-done.1 = f32[3,1,128,1536]{3,2,0,1:T(8,128)S(1)} collective-permute-done((f32[3,1,128,1536]{3,2,0,1:T(8,128)S(1)}, f32[3,1,128,1536]{3,2,0,1:T(8,128)S(1)}, u32[]{:S(2)}, u32[]{:S(2)}) %collective-permute-start.1) | collective-permute-done | bytes 2359328 | tf_op jit(solution)/shard_map/ppermute | solution.py:20
  214.7 71.9 %collective-permute-done.2 = f32[3,1,128,1536]{3,2,0,1:T(8,128)S(1)} collective-permute-done((f32[3,1,128,1536]{3,2,0,1:T(8,128)S(1)}, f32[3,1,128,1536]{3,2,0,1:T(8,128)S(1)}, u32[]{:S(2)}, u32[]{:S(2)}) %collective-permute-start.2) | collective-permute-done | bytes 2359328 | tf_op jit(solution)/shard_map/ppermute | solution.py:20
  286.8 50.4 %collective-permute-done.3 = f32[3,1,128,1536]{3,2,0,1:T(8,128)S(1)} collective-permute-done((f32[3,1,128,1536]{3,2,0,1:T(8,128)S(1)}, f32[3,1,128,1536]{3,2,0,1:T(8,128)S(1)}, u32[]{:S(2)}, u32[]{:S(2)}) %collective-permute-start.3) | collective-permute-done | bytes 2359328 | tf_op jit(solution)/shard_map/ppermute | solution.py:20
  337.3 53.7 %collective-permute-done.4 = f32[3,1,128,1536]{3,2,0,1:T(8,128)S(1)} collective-permute-done((f32[3,1,128,1536]{3,2,0,1:T(8,128)S(1)}, f32[3,1,128,1536]{3,2,0,1:T(8,128)S(1)}, u32[]{:S(2)}, u32[]{:S(2)}) %collective-permute-start.4) | collective-permute-done | bytes 2359328 | tf_op jit(solution)/shard_map/ppermute | solution.py:20
  391.2 1.9 multiply_subtract_fusion.2
  393.8 0.7 pad_maximum_fusion
  394.5 3.1 slice_bitcast_fusion
  (28 shorter events, 3.1 us)
Async XLA Ops:
  0.6 3.4 copy-start.3
  0.6 110.8 %copy-start.4 = (s32[28]{0:T(128)S(1)}, s32[28]{0:T(128)}, u32[]{:S(2)}) copy-start(s32[28]{0:T(128)} %param.7) | copy-start | bytes 340
  0.7 121.3 %copy-start = (f32[1,128,1536]{2,1,0:T(8,128)S(1)}, f32[1,128,1536]{2,1,0:T(8,128)}, u32[]{:S(2)}) copy-start(f32[1,128,1536]{2,1,0:T(8,128)} %param.10) | copy-start | bytes 2359300
  0.7 121.3 %copy-start.1 = (f32[1,128,1536]{2,1,0:T(8,128)S(1)}, f32[1,128,1536]{2,1,0:T(8,128)}, u32[]{:S(2)}) copy-start(f32[1,128,1536]{2,1,0:T(8,128)} %param.9) | copy-start | bytes 2359300
  0.7 121.3 %copy-start.2 = (f32[1,128,1536]{2,1,0:T(8,128)S(1)}, f32[1,128,1536]{2,1,0:T(8,128)}, u32[]{:S(2)}) copy-start(f32[1,128,1536]{2,1,0:T(8,128)} %param.8) | copy-start | bytes 2359300
  4.0 118.0 %collective-permute-start = (f32[3,1,128,1536]{3,2,0,1:T(8,128)}, f32[3,1,128,1536]{3,2,0,1:T(8,128)}, u32[]{:S(2)}, u32[]{:S(2)}) collective-permute-start(f32[3,1,128,1536]{3,2,0,1:T(8,128)} %pad_maximum_fusion.1), channel_id=1, source_target_pairs={{0,224},{32,0},{64,32},{96,64},{128,96},{160,128},{192,160},{224,1... | collective-permute-start | bytes 7077896 | tf_op jit(solution)/shard_map/ppermute | solution.py:26
  4.0 120.6 %collective-permute-start.5 = (bf16[1,128,1536]{2,1,0:T(8,128)(2,1)S(1)}, bf16[1,128,1536]{2,1,0:T(8,128)(2,1)}, u32[]{:S(2)}, u32[]{:S(2)}) collective-permute-start(bf16[1,128,1536]{2,1,0:T(8,128)(2,1)S(1)} %copy-done.3), channel_id=1, source_target_pairs={{1,0},{2,1},{3,2},{4,3},{5,4},{6,5},{7,6},{8,7},{9,8},{10,9},{11,1... | collective-permute-start | bytes 1179656 | tf_op jit(solution)/shard_map/ppermute | solution.py:20
  9.1 122.8 %collective-permute-start.6 = (bf16[1,128,1536]{2,1,0:T(8,128)(2,1)S(1)}, bf16[1,128,1536]{2,1,0:T(8,128)(2,1)}, u32[]{:S(2)}, u32[]{:S(2)}) collective-permute-start(bf16[1,128,1536]{2,1,0:T(8,128)(2,1)S(1)} %copy-done.3), channel_id=1, source_target_pairs={{2,0},{3,1},{4,2},{5,3},{6,4},{7,5},{8,6},{9,7},{10,8},{11,9},{12,... | collective-permute-start | bytes 1179656 | tf_op jit(solution)/shard_map/ppermute | solution.py:20
  11.8 126.3 %collective-permute-start.7 = (bf16[1,128,1536]{2,1,0:T(8,128)(2,1)S(1)}, bf16[1,128,1536]{2,1,0:T(8,128)(2,1)S(1)}, u32[]{:S(2)}, u32[]{:S(2)}) collective-permute-start(bf16[1,128,1536]{2,1,0:T(8,128)(2,1)S(1)} %copy-done.3), channel_id=1, source_target_pairs={{3,0},{4,1},{5,2},{6,3},{7,4},{8,5},{9,6},{10,7},{11,8},{12,9},{13... | collective-permute-start | bytes 1179656 | tf_op jit(solution)/shard_map/ppermute | solution.py:20
  15.0 125.2 %collective-permute-start.8 = (bf16[1,128,1536]{2,1,0:T(8,128)(2,1)S(1)}, bf16[1,128,1536]{2,1,0:T(8,128)(2,1)S(1)}, u32[]{:S(2)}, u32[]{:S(2)}) collective-permute-start(bf16[1,128,1536]{2,1,0:T(8,128)(2,1)S(1)} %copy-done.3), channel_id=1, source_target_pairs={{4,0},{5,1},{6,2},{7,3},{8,4},{9,5},{10,6},{11,7},{12,8},{13,9},{1... | collective-permute-start | bytes 1179656 | tf_op jit(solution)/shard_map/ppermute | solution.py:20
  122.6 91.9 %collective-permute-start.1 = (f32[3,1,128,1536]{3,2,0,1:T(8,128)S(1)}, f32[3,1,128,1536]{3,2,0,1:T(8,128)S(1)}, u32[]{:S(2)}, u32[]{:S(2)}) collective-permute-start(f32[3,1,128,1536]{3,2,0,1:T(8,128)S(1)} %get-tuple-element.15), channel_id=1, source_target_pairs={{1,0},{2,1},{3,2},{4,3},{5,4},{6,5},{7,6},{8,7},{9,8},{10,9},{11,1... | collective-permute-start | bytes 7077896 | tf_op jit(solution)/shard_map/ppermute | solution.py:20
  124.6 162.0 %collective-permute-start.2 = (f32[3,1,128,1536]{3,2,0,1:T(8,128)S(1)}, f32[3,1,128,1536]{3,2,0,1:T(8,128)S(1)}, u32[]{:S(2)}, u32[]{:S(2)}) collective-permute-start(f32[3,1,128,1536]{3,2,0,1:T(8,128)S(1)} %get-tuple-element.15), channel_id=1, source_target_pairs={{2,0},{3,1},{4,2},{5,3},{6,4},{7,5},{8,6},{9,7},{10,8},{11,9},{12,... | collective-permute-start | bytes 7077896 | tf_op jit(solution)/shard_map/ppermute | solution.py:20
  131.9 205.2 %collective-permute-start.3 = (f32[3,1,128,1536]{3,2,0,1:T(8,128)S(1)}, f32[3,1,128,1536]{3,2,0,1:T(8,128)S(1)}, u32[]{:S(2)}, u32[]{:S(2)}) collective-permute-start(f32[3,1,128,1536]{3,2,0,1:T(8,128)S(1)} %get-tuple-element.15), channel_id=1, source_target_pairs={{3,0},{4,1},{5,2},{6,3},{7,4},{8,5},{9,6},{10,7},{11,8},{12,9},{13... | collective-permute-start | bytes 7077896 | tf_op jit(solution)/shard_map/ppermute | solution.py:20
  138.2 252.8 %collective-permute-start.4 = (f32[3,1,128,1536]{3,2,0,1:T(8,128)S(1)}, f32[3,1,128,1536]{3,2,0,1:T(8,128)S(1)}, u32[]{:S(2)}, u32[]{:S(2)}) collective-permute-start(f32[3,1,128,1536]{3,2,0,1:T(8,128)S(1)} %get-tuple-element.15), channel_id=1, source_target_pairs={{4,0},{5,1},{6,2},{7,3},{8,4},{9,5},{10,6},{11,7},{12,8},{13,9},{1... | collective-permute-start | bytes 7077896 | tf_op jit(solution)/shard_map/ppermute | solution.py:20
where the time goes:
time: 398 us
  waiting for transfers between devices  250 us (63%)
  blocking collectives  94.5 us (24%)
  starting transfers between devices  27.5 us (7%)
  other arithmetic  12.1 us (3%)
  local copies, waits for them, and re-layouts  7.14 us (2%)
  between operations  6.09 us (2%)
    ppermute x8, waiting for transfers between devices, shifted(): lax.ppermute(value, axis, [(source, source + steps) for source in range(i...  250 us
    psum x1, blocking collectives, on_device(): norm_sum = lax.psum(local_sum, 'wide')  94.5 us
    ppermute x8, starting transfers between devices, shifted(): lax.ppermute(value, axis, [(source, source + steps) for source in range(i...  27.5 us
  transfers between devices with their start and end apart: 9, of which 4 were waited for; matrix products, arithmetic and copies ran while one was open for 2% of the time, Pallas kernels for 0%

commit v1 on v0

v1 whole, which is shorter than its diff:
```python
import functools
import math

import jax
import jax.numpy as jnp
from jax import lax
from jax.experimental import pallas as pl
from jax.experimental.pallas import tpu as pltpu
from jax.sharding import PartitionSpec as P

beta_first = 0.9
beta_second = 0.95
bias_first = 1.0 - 0.9**20
bias_second = 1.0 - 0.95**20
learn_rate = 0.01
weight_decay = 0.1
eps_adam = 1e-08

WIDE = 32
REP = 8
SHIFT = 4
SLOTS = 3
STAGE_TWO = tuple(range(4, WIDE, 4))
MESH = pl.DeviceIdType.MESH


def gather_kernel(
    lost_ref, blocks_ref, w_ref, m_ref, v_ref, g_ref,
    gat_ref, gwin_ref, norm_ref, meta_ref,
    own, fix, win_w, win_m, win_v, sel, gv, part_one, part_two,
    loc, fix_s, fix_r, win_s, win_r, g_s, g_r, one_s, one_r, two_s, two_r, y_s, y_r, c_s, c_r,
):
    arrays = (w_ref, m_ref, v_ref)
    wins = (win_w, win_m, win_v)
    rows = own.shape[1]
    island = lax.axis_index("rep")
    shard = lax.axis_index("wide")
    partner = island + 1 - 2 * lax.rem(island, 2)

    def lower(d):
        return {"rep": island, "wide": lax.rem(shard + WIDE - d, WIDE)}

    def higher(d):
        return {"rep": island, "wide": lax.rem(shard + d, WIDE)}

    def along_y(dy):
        return lax.rem(island + 2 * dy, REP)

    def piece(p):
        return pl.ds(pl.multiple_of(p * rows, rows), rows)

    def remote(src, dst, s, r, where):
        return pltpu.make_async_remote_copy(src, dst, s, r, device_id=where, device_id_type=MESH)

    to_partner = {"rep": partner, "wide": shard}

    own_in = [pltpu.make_async_copy(arrays[a].at[piece(island)], own.at[a], loc.at[a]) for a in range(3)]
    grad_in = pltpu.make_async_copy(g_ref, gv, loc.at[3])
    grad_own = pltpu.make_async_copy(g_ref, gwin_ref.at[0], loc.at[4])
    grad_in.start()
    for copy in own_in:
        copy.start()

    barrier = pltpu.get_barrier_semaphore()
    offsets = (1, 2, 3, *STAGE_TWO)
    for d in offsets:
        pl.semaphore_signal(barrier, inc=1, device_id=higher(d), device_id_type=MESH)
    for dy in range(1, 4):
        pl.semaphore_signal(barrier, inc=1, device_id={"rep": along_y(dy), "wide": shard}, device_id_type=MESH)
    pl.semaphore_signal(barrier, inc=1, device_id=to_partner, device_id_type=MESH)
    pl.semaphore_wait(barrier, len(offsets) + 4)

    mend = [remote(arrays[a].at[piece(partner)], fix.at[a], fix_s.at[a], fix_r.at[a], to_partner) for a in range(3)]
    for copy in mend:
        copy.start()

    grad_in.wait()
    grad_own.start()
    step = 16

    def add_rows(i, total):
        x = gv[pl.ds(pl.multiple_of(i * step, step), step), :].astype(jnp.float32)
        return total + fold(x * x)

    def fold(sq):
        top = sq[:8] + sq[8:]
        parts = [top[:, 128 * c : 128 * (c + 1)] for c in range(top.shape[1] // 128)]
        while len(parts) > 1:
            parts = [sum(parts[i : i + 2][1:], parts[i]) for i in range(0, len(parts), 2)]
        return parts[0]

    part_one[0] = lax.fori_loop(0, gv.shape[0] // step, add_rows, jnp.zeros((8, 128), jnp.float32))
    ones = [remote(part_one.at[0], part_one.at[d], one_s.at[d - 1], one_r.at[d - 1], lower(d)) for d in range(1, 4)]
    for copy in ones:
        copy.start()

    first = jnp.int32(0)
    count = jnp.int32(0)
    for k in range(blocks_ref.shape[0]):
        n = blocks_ref[k]
        first = first + jnp.where(k < shard, n, 0)
        count = count + jnp.where(k == shard, n, 0)
    gaps = [jnp.clip(first + s - shard, 0, SHIFT) for s in range(SLOTS)]
    meta_ref[0] = count
    for s in range(SLOTS):
        meta_ref[1 + s] = gaps[s]
    broken = lost_ref[island] == shard

    windows = []
    for a in range(3):
        own_in[a].wait()
        mend[a].wait_recv()
        wins[a][0] = jnp.where(broken, fix[a], own[a])
        sends = [
            remote(wins[a].at[0], wins[a].at[d], win_s.at[a, d - 1], win_r.at[a, d - 1], lower(d))
            for d in range(1, SHIFT + 1)
        ]
        for copy in sends:
            copy.start()
        windows.append(sends)

    grads = [remote(g_ref, gwin_ref.at[d], g_s.at[d - 1], g_r.at[d - 1], lower(d)) for d in range(1, SHIFT + 1)]
    for copy in grads:
        copy.start()

    for copy in ones:
        copy.wait_recv()
    part_two[0] = part_one[0] + part_one[1] + part_one[2] + part_one[3]
    twos = [
        remote(part_two.at[0], part_two.at[k + 1], two_s.at[k], two_r.at[k], lower(d))
        for k, d in enumerate(STAGE_TWO)
    ]
    for copy in twos:
        copy.start()

    kept, crossed, passed = [], [], []
    for a in range(3):
        for copy in windows[a]:
            copy.wait_recv()
        for s in range(SLOTS):
            sel[a, s] = wins[a][gaps[s]]
        mine = gat_ref.at[a, :, piece(island)]
        keep = pltpu.make_async_copy(sel.at[a], mine, loc.at[5 + a])
        sends = [
            remote(sel.at[a], mine, y_s.at[a, dy - 1], y_r.at[a, dy - 1], {"rep": along_y(dy), "wide": shard})
            for dy in range(1, 4)
        ]
        over = remote(sel.at[a], mine, c_s.at[a, 0], c_r.at[a, 0], to_partner)
        for copy in (*sends, over, keep):
            copy.start()
        kept.append(keep)
        crossed.append(sends)
        passed.append([over])
    for a in range(3):
        for dy in range(1, 4):
            theirs = gat_ref.at[a, :, piece(lax.rem(island + REP - 2 * dy, REP))]
            remote(sel.at[a], theirs, y_s.at[a, dy - 1], y_r.at[a, dy - 1], to_partner).wait_recv()
            over = remote(theirs, theirs, c_s.at[a, dy], c_r.at[a, dy], to_partner)
            over.start()
            passed[a].append(over)

    for copy in twos:
        copy.wait_recv()
    total = part_two[0]
    for k in range(1, len(STAGE_TWO) + 1):
        total = total + part_two[k]
    norm_ref[...] = total

    for copy in (*mend, *ones, *twos):
        copy.wait_send()
    grad_own.wait()
    for copy in grads:
        copy.wait()
    for a in range(3):
        kept[a].wait()
        for copy in (*windows[a], *crossed[a]):
            copy.wait_send()
        for copy in passed[a]:
            copy.wait()


def update_kernel(limit, meta_ref, norm_ref, gat_ref, g_ref, w_out, m_out, v_out, factor_ref):
    slot, part = pl.program_id(0), pl.program_id(1)

    @pl.when(jnp.logical_and(slot == 0, part == 0))
    def _():
        norm_sum = jnp.sum(norm_ref[...], keepdims=True)
        factor_ref[...] = jnp.broadcast_to(jnp.minimum(1.0, limit / (jnp.sqrt(norm_sum) + 1e-06)), factor_ref.shape)

    @pl.when(slot < meta_ref[0])
    def _():
        factor = factor_ref[0:1, 0:1]
        params, moment_one, moment_two = gat_ref[0, 0], gat_ref[1, 0], gat_ref[2, 0]
        clipped = g_ref[0].astype(jnp.float32) * factor
        one_new = beta_first * moment_one + (1.0 - beta_first) * clipped
        two_new = beta_second * moment_two + (1.0 - beta_second) * clipped * clipped
        step_dir = one_new / bias_first / (jnp.sqrt(two_new / bias_second) + eps_adam)
        w_out[...] = params - learn_rate * (step_dir + weight_decay * params)
        m_out[...] = one_new
        v_out[...] = two_new

    @pl.when(slot >= meta_ref[0])
    def _():
        for out in (w_out, m_out, v_out):
            out[...] = jnp.zeros_like(out)


def on_device(shard_lost, new_blocks, weights, first_moment, second_moment, gradient):
    _, block, ff = weights.shape
    rows = block // REP
    f32 = jnp.float32
    vmem, anywhere = pl.BlockSpec(memory_space=pltpu.VMEM), pl.BlockSpec(memory_space=pl.ANY)
    smem = pl.BlockSpec(memory_space=pltpu.SMEM)
    dma = lambda *shape: pltpu.SemaphoreType.DMA(shape)
    gat, gwin, norm, meta = pl.pallas_call(
        gather_kernel,
        out_shape=(
            jax.ShapeDtypeStruct((3, SLOTS, block, ff), f32),
            jax.ShapeDtypeStruct((SHIFT + 1, block, ff), jnp.bfloat16),
            jax.ShapeDtypeStruct((8, 128), f32),
            jax.ShapeDtypeStruct((8,), jnp.int32),
        ),
        in_specs=[smem, smem] + [anywhere] * 4,
        out_specs=(anywhere, anywhere, vmem, smem),
        scratch_shapes=[
            pltpu.VMEM((3, rows, ff), f32),
            pltpu.VMEM((3, rows, ff), f32),
            *[pltpu.VMEM((SHIFT + 1, rows, ff), f32)] * 3,
            pltpu.VMEM((3, SLOTS, rows, ff), f32),
            pltpu.VMEM((block, ff), jnp.bfloat16),
            pltpu.VMEM((4, 8, 128), f32),
            pltpu.VMEM((8, 8, 128), f32),
            dma(8), dma(3), dma(3), dma(3, 4), dma(3, 4), dma(4), dma(4),
            dma(3), dma(3), dma(7), dma(7), dma(3, 3), dma(3, 3), dma(3, 4), dma(3, 4),
        ],
        compiler_params=pltpu.CompilerParams(
            collective_id=0, has_side_effects=True, vmem_limit_bytes=24 * 2**20
        ),
        name="gather_blocks",
    )(shard_lost, new_blocks, weights[0], first_moment[0], second_moment[0], gradient[0])

    chunk = 64
    parts = block // chunk

    def source(slot, part, meta_ref):
        last = jnp.maximum(meta_ref[0], 1) - 1
        return jnp.minimum(slot, last), jnp.where(slot > last, parts - 1, part)

    def gat_map(slot, part, meta_ref):
        s, i = source(slot, part, meta_ref)
        return 0, s, i, 0

    def grad_map(slot, part, meta_ref):
        s, i = source(slot, part, meta_ref)
        return meta_ref[1 + s], i, 0

    out_spec = pl.BlockSpec((chunk, ff), lambda slot, part, meta_ref: (slot * parts + part, 0))
    limit = 0.5 * math.sqrt(block * WIDE * ff)
    outs = pl.pallas_call(
        functools.partial(update_kernel, limit),
        out_shape=[jax.ShapeDtypeStruct((SLOTS * block, ff), f32)] * 3,
        grid_spec=pltpu.PrefetchScalarGridSpec(
            num_scalar_prefetch=1,
            grid=(SLOTS, parts),
            in_specs=[
                pl.BlockSpec((8, 128), lambda slot, part, meta_ref: (0, 0)),
                pl.BlockSpec((3, 1, chunk, ff), gat_map),
                pl.BlockSpec((1, chunk, ff), grad_map),
            ],
            out_specs=[out_spec] * 3,
            scratch_shapes=[pltpu.VMEM((8, 128), f32)],
        ),
        compiler_params=pltpu.CompilerParams(vmem_limit_bytes=24 * 2**20),
        name="adam_update",
    )(meta, norm, gat, gwin)
    return tuple(out[None] for out in outs)


def solution(mesh):
    split = P("rep", "wide", None)
    return jax.shard_map(
        on_device,
        mesh=mesh,
        in_specs=(P(), P(), split, split, split, split),
        out_specs=(split, split, split),
        check_vma=False,
    )
```

time: 398 us -> 90.7 us (0.23)
  the two profiles are of different devices: /device:TPU:176 before, /device:TPU:1 now
where the time goes in v1:
time: 90.7 us; the launch traced here: 90.4 us
  Pallas kernels  84.1 us (93%)
  local copies, waits for them, and re-layouts  5.7 us (6%)
    pallas_call x1, Pallas kernels, on_device(): pl.pallas_call(gather_kernel, out_shape=(jax.ShapeDtypeStruct((3, SLOTS,...  78 us
    pallas_call x1, Pallas kernels, on_device(): pl.pallas_call(functools.partial(update_kernel, limit), out_shape=[jax.Sh...  6.08 us
    unnamed x12, local copies, waits for them, and re-layouts  5.7 us

profile of v1, /device:TPU:1, one launch (start us, length us, event | category | flops | bytes accessed | tf_op | source)
XLA Modules:
  0.0 90.4 jit_solution(2677245698476685623)
XLA Ops:
  0.6 0.0 copy-start
  0.6 1.1 %copy-done = f32[1,128,1536]{2,1,0:T(8,128)S(1)} copy-done((f32[1,128,1536]{2,1,0:T(8,128)S(1)}, f32[1,128,1536]{2,1,0:T(8,128)}, u32[]{:S(2)}) %copy-start) | copy-done | bytes 786456
  1.8 0.0 copy-start.1
  1.8 1.1 %copy-done.1 = f32[1,128,1536]{2,1,0:T(8,128)S(1)} copy-done((f32[1,128,1536]{2,1,0:T(8,128)S(1)}, f32[1,128,1536]{2,1,0:T(8,128)}, u32[]{:S(2)}) %copy-start.1) | copy-done | bytes 786456
  2.9 0.0 copy-start.2
  2.9 1.1 %copy-done.2 = f32[1,128,1536]{2,1,0:T(8,128)S(1)} copy-done((f32[1,128,1536]{2,1,0:T(8,128)S(1)}, f32[1,128,1536]{2,1,0:T(8,128)}, u32[]{:S(2)}) %copy-start.2) | copy-done | bytes 786456
  4.0 0.0 copy-start.3
  4.0 1.0 %copy-done.3 = bf16[1,128,1536]{2,1,0:T(8,128)(2,1)S(1)} copy-done((bf16[1,128,1536]{2,1,0:T(8,128)(2,1)S(1)}, bf16[1,128,1536]{2,1,0:T(8,128)(2,1)}, u32[]{:S(2)}) %copy-start.3) | copy-done | bytes 393240
  5.0 0.0 copy-start.4
  5.0 0.7 copy-done.4
  5.7 0.0 copy-start.5
  5.7 0.7 copy-done.5
  6.3 78.0 %gather_blocks.1 = (f32[3,3,128,1536]{3,2,1,0:T(8,128)S(1)}, bf16[5,128,1536]{2,1,0:T(8,128)(2,1)S(1)}, f32[8,128]{1,0:T(8,128)S(1)}, s32[8]{0:T(128)S(1)}) custom-call(s32[8]{0:T(128)S(1)} %copy-done.4, s32[28]{0:T(128)S(1)} %copy-done.5, f32[128,1536]{1,0:T(8,128)S(1)} %bitcast.7, f32[128,1536]{1,0:T(8,128)S(1)} %bitcast.8, f32[128,1536]{1,0:T(8,128)S(1)} %bitcast.9, ...), custom_call_target="tpu_custom_call" | custom-call | tf_op jit(solution)/shard_map/gather_blocks/pallas_call | solution.py:215
  84.3 6.1 %adam_update.1 = (f32[384,1536]{1,0:T(8,128)}, f32[384,1536]{1,0:T(8,128)}, f32[384,1536]{1,0:T(8,128)}) custom-call(s32[8]{0:T(128)S(1)} %get-tuple-element.10.meta_ref, f32[8,128]{1,0:T(8,128)S(1)} %get-tuple-element.11.norm_ref, f32[3,3,128,1536]{3,2,1,0:T(8,128)S(1)} %get-tuple-element.12.gat_ref, bf16[5,128,1536]{2,1,0:T(8,128)(2,1)S(1)} %get-tuple-element.13.g_ref), custom_call_target="tpu_custom_call" | custom-call | tf_op jit(solution)/shard_map/adam_update/pallas_call | solution.py:259
Async XLA Ops:
  0.6 1.1 %copy-start = (f32[1,128,1536]{2,1,0:T(8,128)S(1)}, f32[1,128,1536]{2,1,0:T(8,128)}, u32[]{:S(2)}) copy-start(f32[1,128,1536]{2,1,0:T(8,128)} %param.8) | copy-start | bytes 2359300
  1.8 1.1 %copy-start.1 = (f32[1,128,1536]{2,1,0:T(8,128)S(1)}, f32[1,128,1536]{2,1,0:T(8,128)}, u32[]{:S(2)}) copy-start(f32[1,128,1536]{2,1,0:T(8,128)} %param.9) | copy-start | bytes 2359300
  2.9 1.1 %copy-start.2 = (f32[1,128,1536]{2,1,0:T(8,128)S(1)}, f32[1,128,1536]{2,1,0:T(8,128)}, u32[]{:S(2)}) copy-start(f32[1,128,1536]{2,1,0:T(8,128)} %param.10) | copy-start | bytes 2359300
  4.0 1.0 %copy-start.3 = (bf16[1,128,1536]{2,1,0:T(8,128)(2,1)S(1)}, bf16[1,128,1536]{2,1,0:T(8,128)(2,1)}, u32[]{:S(2)}) copy-start(bf16[1,128,1536]{2,1,0:T(8,128)(2,1)} %param.11) | copy-start | bytes 1179652
  5.0 0.7 copy-start.4
  5.7 0.7 copy-start.5

commit v2 on v1

v2 whole, which is shorter than its diff:
```python
import functools
import math

import jax
import jax.numpy as jnp
from jax import lax
from jax.experimental import pallas as pl
from jax.experimental.pallas import tpu as pltpu
from jax.sharding import PartitionSpec as P

beta_first = 0.9
beta_second = 0.95
bias_first = 1.0 - 0.9**20
bias_second = 1.0 - 0.95**20
learn_rate = 0.01
weight_decay = 0.1
eps_adam = 1e-08

WIDE = 32
REP = 8
SHIFT = 4
SLOTS = 3
LANES = 128
TOP = 32767.0
CHUNKS = 4
STAGE_TWO = tuple(range(4, WIDE, 4))
MESH = pl.DeviceIdType.MESH


def encode(x, out):
    size = jnp.abs(x)
    most = jnp.clip(jnp.max(size, axis=1, keepdims=True), 2.0**-120, 2.0**120)
    exponent = jnp.ceil(jnp.log2(most))
    code = jnp.minimum(jnp.round(jnp.sqrt(size * jnp.exp2(-exponent)) * TOP), TOP)
    code = jnp.where(x < 0, -code, code)
    out[:, : x.shape[1]] = code.astype(jnp.int32).astype(jnp.int16)
    tail = jnp.broadcast_to(exponent, (x.shape[0], LANES))
    out[:, x.shape[1] :] = tail.astype(jnp.int32).astype(jnp.int16)


def decode(x):
    columns = x.shape[1] - LANES
    code = x[:, :columns].astype(jnp.int32).astype(jnp.float32)
    scale = jnp.exp2(x[:, columns:].astype(jnp.int32).astype(jnp.float32)) * (1.0 / TOP**2)
    return code * jnp.abs(code) * jnp.concatenate([scale] * (columns // LANES), axis=1)


def fold(squares):
    top = squares[:8] + squares[8:]
    parts = [top[:, LANES * c : LANES * (c + 1)] for c in range(top.shape[1] // LANES)]
    while len(parts) > 1:
        parts = [sum(parts[i : i + 2][1:], parts[i]) for i in range(0, len(parts), 2)]
    return parts[0]


def gather_kernel(
    lost_hbm, blocks_hbm, w_ref, m_ref, v_ref, g_ref,
    gat_ref, gwin_ref, norm_ref, meta_ref,
    lost_ref, blocks_ref, own, fix, win_w, win_m, win_v, sel, gv, part_one, part_two, loc, out_sem, in_sem,
):
    arrays = (w_ref, m_ref, v_ref)
    wins = (win_w, win_m, win_v)
    rows = own.shape[1]
    island = lax.axis_index("rep")
    shard = lax.axis_index("wide")
    partner = island + 1 - 2 * lax.rem(island, 2)
    width = sel.shape[3]
    middle = width // LANES // 2 * LANES
    left, right = pl.ds(0, middle), pl.ds(middle, width - middle)
    to_partner = {"rep": partner, "wide": shard}
    used = {"remote": 0, "local": 0}

    def lower(d):
        return {"rep": island, "wide": lax.rem(shard + WIDE - d, WIDE)}

    def higher(d):
        return {"rep": island, "wide": lax.rem(shard + d, WIDE)}

    def along_y(dy):
        return lax.rem(island + REP + 2 * dy, REP)

    def chip_y(dy):
        return {"rep": along_y(dy), "wide": shard}

    def piece(p):
        return pl.ds(pl.multiple_of(p * rows, rows), rows)

    def send(src, dst, where, lands=None):
        k = used["remote"]
        used["remote"] = k + 1
        copy = pltpu.make_async_remote_copy(src, dst, out_sem.at[k], in_sem.at[k], device_id=where, device_id_type=MESH)
        copy.start()
        if lands is None:
            return copy, copy
        return copy, pltpu.make_async_remote_copy(
            src, lands, out_sem.at[k], in_sem.at[k], device_id=where, device_id_type=MESH
        )

    def local(src, dst):
        k = used["local"]
        used["local"] = k + 1
        copy = pltpu.make_async_copy(src, dst, loc.at[k])
        copy.start()
        return copy

    sent, kept = [], []

    def ship(*args, **kwargs):
        copy, lands = send(*args, **kwargs)
        sent.append(copy)
        return lands

    grad_in = local(g_ref, gv)
    own_in = [local(arrays[a].at[piece(island)], own.at[a]) for a in range(3)]
    lost_in, blocks_in = local(lost_hbm, lost_ref), local(blocks_hbm, blocks_ref)

    barrier = pltpu.get_barrier_semaphore()
    offsets = (1, 2, 3, *STAGE_TWO, WIDE - 1)
    greeted = [*(higher(d) for d in offsets), chip_y(1), chip_y(-1), to_partner]
    for device in greeted:
        pl.semaphore_signal(barrier, inc=1, device_id=device, device_id_type=MESH)
    pl.semaphore_wait(barrier, len(greeted))

    mend = [ship(arrays[a].at[piece(partner)], fix.at[a], to_partner) for a in range(3)]

    gstep = gv.shape[0] // CHUNKS
    gone = [pl.ds(c * gstep, gstep) for c in range(CHUNKS)]
    grad_four, grad_one = [], []

    def send_gradient(c):
        grad_four.append(ship(g_ref.at[gone[c]], gwin_ref.at[4, gone[c]], lower(4)))
        grad_one.append(ship(g_ref.at[gone[c]], gwin_ref.at[1, gone[c]], lower(1)))

    send_gradient(0)

    lost_in.wait()
    blocks_in.wait()
    first = jnp.int32(0)
    count = jnp.int32(0)
    for k in range(blocks_ref.shape[0]):
        n = blocks_ref[k]
        first = first + jnp.where(k < shard, n, 0)
        count = count + jnp.where(k == shard, n, 0)
    gaps = [jnp.clip(first + s - shard, 0, SHIFT) for s in range(SLOTS)]
    meta_ref[0] = count
    for s in range(SLOTS):
        meta_ref[1 + s] = gaps[s]
    broken = lost_ref[island] == shard

    got = []
    for a in range(3):
        own_in[a].wait()
        mend[a].wait_recv()
        encode(jnp.where(broken, fix[a], own[a]), wins[a].at[0])
        got.append({d: ship(wins[a].at[0], wins[a].at[d], lower(d)) for d in (1, 3, 4)})

    grad_in.wait()
    kept.append(local(gv, gwin_ref.at[0]))
    step = 16

    def add_rows(i, total):
        x = gv[pl.ds(pl.multiple_of(i * step, step), step), :].astype(jnp.float32)
        return total + fold(x * x)

    part_one[0] = lax.fori_loop(0, gv.shape[0] // step, add_rows, jnp.zeros((8, LANES), jnp.float32))
    ones = [ship(part_one.at[0], part_one.at[d], lower(d)) for d in range(1, 4)]

    for c in range(1, CHUNKS):
        send_gradient(c)

    for a in range(3):
        got[a][1].wait_recv()
        got[a][2] = ship(wins[a].at[1, :, left], wins[a].at[2, :, left], lower(1))
        got[a][3].wait_recv()
        got[a][5] = ship(wins[a].at[3, :, right], wins[a].at[2, :, right], higher(1))

    for copy in ones:
        copy.wait_recv()
    part_two[0] = part_one[0] + part_one[1] + part_one[2] + part_one[3]
    twos = [ship(part_two.at[0], part_two.at[k + 1], lower(d)) for k, d in enumerate(STAGE_TWO)]

    up, down, across = [], [], []
    for a in range(3):
        for d in (4, 2, 5):
            got[a][d].wait_recv()
        for s in range(SLOTS):
            sel[a, s] = wins[a][gaps[s]]
        mine = gat_ref.at[a, :, piece(island)]
        up.append(ship(sel.at[a], mine, chip_y(1), lands=gat_ref.at[a, :, piece(along_y(-1))]))
        down.append(ship(sel.at[a], mine, chip_y(-1), lands=gat_ref.at[a, :, piece(along_y(1))]))
        across.append(ship(sel.at[a], mine, to_partner, lands=gat_ref.at[a, :, piece(partner)]))
        kept.append(local(sel.at[a], mine))

    grad_rest, grad_three = [], []
    for c in range(CHUNKS):
        grad_four[c].wait_recv()
        grad_three.append(ship(gwin_ref.at[4, gone[c]], gwin_ref.at[3, gone[c]], higher(1)))
        grad_one[c].wait_recv()
        if c < CHUNKS // 2:
            grad_rest.append(ship(gwin_ref.at[1, gone[c]], gwin_ref.at[2, gone[c]], lower(1)))

    partner_y = [lax.rem(partner + REP + 2 * dy, REP) for dy in range(4)]

    def cross(a, dy):
        theirs = gat_ref.at[a, :, piece(along_y(dy))]
        across.append(ship(theirs, theirs, to_partner, lands=gat_ref.at[a, :, piece(partner_y[dy])]))

    far = []
    for a in range(3):
        up[a].wait_recv()
        theirs = gat_ref.at[a, :, piece(along_y(-1)), left]
        far.append(ship(theirs, theirs, chip_y(1), lands=gat_ref.at[a, :, piece(along_y(2)), left]))
        down[a].wait_recv()
        theirs = gat_ref.at[a, :, piece(along_y(1)), right]
        far.append(ship(theirs, theirs, chip_y(-1), lands=gat_ref.at[a, :, piece(along_y(2)), right]))
        cross(a, 3)
        cross(a, 1)
    for c in range(CHUNKS):
        grad_three[c].wait_recv()
        if c >= CHUNKS // 2:
            grad_rest.append(ship(gwin_ref.at[3, gone[c]], gwin_ref.at[2, gone[c]], higher(1)))
    for a in range(3):
        far[2 * a].wait_recv()
        far[2 * a + 1].wait_recv()
        cross(a, 2)

    for copy in twos:
        copy.wait_recv()
    total = part_two[0]
    for k in range(1, len(STAGE_TWO) + 1):
        total = total + part_two[k]
    norm_ref[...] = total

    for copy in (*grad_rest, *across):
        copy.wait_recv()
    for copy in sent:
        copy.wait_send()
    for copy in kept:
        copy.wait()


def update_kernel(limit, meta_ref, norm_ref, gat_ref, g_ref, w_out, m_out, v_out, factor_ref):
    slot, part = pl.program_id(0), pl.program_id(1)

    @pl.when(jnp.logical_and(slot == 0, part == 0))
    def _():
        norm_sum = jnp.sum(norm_ref[...], keepdims=True)
        factor_ref[...] = jnp.broadcast_to(jnp.minimum(1.0, limit / (jnp.sqrt(norm_sum) + 1e-06)), factor_ref.shape)

    @pl.when(slot < meta_ref[0])
    def _():
        factor = factor_ref[0:1, 0:1]
        params, moment_one, moment_two = (decode(gat_ref[a, 0]) for a in range(3))
        clipped = g_ref[0].astype(jnp.float32) * factor
        one_new = beta_first * moment_one + (1.0 - beta_first) * clipped
        two_new = beta_second * moment_two + (1.0 - beta_second) * clipped * clipped
        step_dir = one_new / bias_first / (jnp.sqrt(two_new / bias_second) + eps_adam)
        w_out[...] = params - learn_rate * (step_dir + weight_decay * params)
        m_out[...] = one_new
        v_out[...] = two_new

    @pl.when(slot >= meta_ref[0])
    def _():
        for out in (w_out, m_out, v_out):
            out[...] = jnp.zeros_like(out)


def on_device(shard_lost, new_blocks, weights, first_moment, second_moment, gradient):
    _, block, ff = weights.shape
    rows = block // REP
    width = ff + LANES
    f32 = jnp.float32
    vmem, anywhere = pl.BlockSpec(memory_space=pltpu.VMEM), pl.BlockSpec(memory_space=pl.ANY)
    smem = pl.BlockSpec(memory_space=pltpu.SMEM)
    hbm = pl.BlockSpec(memory_space=pltpu.HBM)
    gat, gwin, norm, meta = pl.pallas_call(
        gather_kernel,
        out_shape=(
            jax.ShapeDtypeStruct((3, SLOTS, block, width), jnp.int16),
            jax.ShapeDtypeStruct((SHIFT + 1, block, ff), jnp.bfloat16),
            jax.ShapeDtypeStruct((8, 128), f32),
            jax.ShapeDtypeStruct((8,), jnp.int32),
        ),
        in_specs=[hbm] * 6,
        out_specs=(anywhere, anywhere, vmem, smem),
        scratch_shapes=[
            pltpu.SMEM(shard_lost.shape, jnp.int32),
            pltpu.SMEM(new_blocks.shape, jnp.int32),
            pltpu.VMEM((3, rows, ff), f32),
            pltpu.VMEM((3, rows, ff), f32),
            *[pltpu.VMEM((SHIFT + 1, rows, width), jnp.int16)] * 3,
            pltpu.VMEM((3, SLOTS, rows, width), jnp.int16),
            pltpu.VMEM((block, ff), jnp.bfloat16),
            pltpu.VMEM((4, 8, LANES), f32),
            pltpu.VMEM((8, 8, LANES), f32),
            pltpu.SemaphoreType.DMA((10,)),
            pltpu.SemaphoreType.DMA((72,)),
            pltpu.SemaphoreType.DMA((72,)),
        ],
        compiler_params=pltpu.CompilerParams(
            collective_id=0, has_side_effects=True, vmem_limit_bytes=24 * 2**20
        ),
        name="gather_blocks",
    )(shard_lost, new_blocks, weights[0], first_moment[0], second_moment[0], gradient[0])

    chunk = 64
    parts = block // chunk

    def source(slot, part, meta_ref):
        last = jnp.maximum(meta_ref[0], 1) - 1
        return jnp.minimum(slot, last), jnp.where(slot > last, parts - 1, part)

    def gat_map(slot, part, meta_ref):
        s, i = source(slot, part, meta_ref)
        return 0, s, i, 0

    def grad_map(slot, part, meta_ref):
        s, i = source(slot, part, meta_ref)
        return meta_ref[1 + s], i, 0

    out_spec = pl.BlockSpec((chunk, ff), lambda slot, part, meta_ref: (slot * parts + part, 0))
    limit = 0.5 * math.sqrt(block * WIDE * ff)
    outs = pl.pallas_call(
        functools.partial(update_kernel, limit),
        out_shape=[jax.ShapeDtypeStruct((SLOTS * block, ff), f32)] * 3,
        grid_spec=pltpu.PrefetchScalarGridSpec(
            num_scalar_prefetch=1,
            grid=(SLOTS, parts),
            in_specs=[
                pl.BlockSpec((8, 128), lambda slot, part, meta_ref: (0, 0)),
                pl.BlockSpec((3, 1, chunk, width), gat_map),
                pl.BlockSpec((1, chunk, ff), grad_map),
            ],
            out_specs=[out_spec] * 3,
            scratch_shapes=[pltpu.VMEM((8, 128), f32)],
        ),
        compiler_params=pltpu.CompilerParams(vmem_limit_bytes=24 * 2**20),
        name="adam_update",
    )(meta, norm, gat, gwin)
    return tuple(out[None] for out in outs)


def solution(mesh):
    split = P("rep", "wide", None)
    return jax.shard_map(
        on_device,
        mesh=mesh,
        in_specs=(P(), P(), split, split, split, split),
        out_specs=(split, split, split),
        check_vma=False,
    )
```

time: 90.7 us -> 76.1 us (0.84)
  the two profiles are of different devices: /device:TPU:1 before, /device:TPU:8 now
where the time goes in v2:
time: 76.1 us; the launch traced here: 75.8 us
  Pallas kernels  69.5 us (91%)
  local copies, waits for them, and re-layouts  5.7 us (7%)
    pallas_call x1, Pallas kernels, on_device(): pl.pallas_call(gather_kernel, out_shape=(jax.ShapeDtypeStruct((3, SLOTS,...  62.8 us
    pallas_call x1, Pallas kernels, on_device(): pl.pallas_call(functools.partial(update_kernel, limit), out_shape=[jax.Sh...  6.69 us
    unnamed x12, local copies, waits for them, and re-layouts  5.7 us

profile of v2, /device:TPU:8, one launch (start us, length us, event | category | flops | bytes accessed | tf_op | source)
XLA Modules:
  0.0 75.8 jit_solution(10293204400027784161)
XLA Ops:
  0.6 0.0 copy-start
  0.6 1.1 %copy-done = f32[1,128,1536]{2,1,0:T(8,128)S(1)} copy-done((f32[1,128,1536]{2,1,0:T(8,128)S(1)}, f32[1,128,1536]{2,1,0:T(8,128)}, u32[]{:S(2)}) %copy-start) | copy-done | bytes 786456
  1.8 0.0 copy-start.1
  1.8 1.1 %copy-done.1 = f32[1,128,1536]{2,1,0:T(8,128)S(1)} copy-done((f32[1,128,1536]{2,1,0:T(8,128)S(1)}, f32[1,128,1536]{2,1,0:T(8,128)}, u32[]{:S(2)}) %copy-start.1) | copy-done | bytes 786456
  2.9 0.0 copy-start.2
  2.9 1.1 %copy-done.2 = f32[1,128,1536]{2,1,0:T(8,128)S(1)} copy-done((f32[1,128,1536]{2,1,0:T(8,128)S(1)}, f32[1,128,1536]{2,1,0:T(8,128)}, u32[]{:S(2)}) %copy-start.2) | copy-done | bytes 786456
  4.0 0.0 copy-start.3
  4.0 1.0 %copy-done.3 = bf16[1,128,1536]{2,1,0:T(8,128)(2,1)S(1)} copy-done((bf16[1,128,1536]{2,1,0:T(8,128)(2,1)S(1)}, bf16[1,128,1536]{2,1,0:T(8,128)(2,1)}, u32[]{:S(2)}) %copy-start.3) | copy-done | bytes 393240
  5.0 0.0 copy-start.4
  5.0 0.7 copy-done.4
  5.7 0.0 copy-start.5
  5.7 0.7 copy-done.5
  6.3 62.8 %gather_blocks.1 = (s16[3,3,128,1664]{3,2,1,0:T(8,128)(2,1)S(1)}, bf16[5,128,1536]{2,1,0:T(8,128)(2,1)S(1)}, f32[8,128]{1,0:T(8,128)S(1)}, s32[8]{0:T(128)S(1)}) custom-call(s32[8]{0:T(128)S(1)} %copy-done.4, s32[28]{0:T(128)S(1)} %copy-done.5, f32[128,1536]{1,0:T(8,128)S(1)} %bitcast.7, f32[128,1536]{1,0:T(8,128)S(1)} %bitcast.8, f32[128,1536]{1,0:T(8,128)S(1)} %bitcast.9, ...), custom_call_target="tpu_custom_call" | custom-call | tf_op jit(solution)/shard_map/gather_blocks/pallas_call | solution.py:276
  69.1 6.7 %adam_update.1 = (f32[384,1536]{1,0:T(8,128)}, f32[384,1536]{1,0:T(8,128)}, f32[384,1536]{1,0:T(8,128)}) custom-call(s32[8]{0:T(128)S(1)} %get-tuple-element.10.meta_ref, f32[8,128]{1,0:T(8,128)S(1)} %get-tuple-element.11.norm_ref, s16[3,3,128,1664]{3,2,1,0:T(8,128)(2,1)S(1)} %get-tuple-element.12.gat_ref, bf16[5,128,1536]{2,1,0:T(8,128)(2,1)S(1)} %get-tuple-element.13.g_ref), custom_call_target="tpu_custom_call" | custom-call | tf_op jit(solution)/shard_map/adam_update/pallas_call | solution.py:323
Async XLA Ops:
  0.6 1.1 %copy-start = (f32[1,128,1536]{2,1,0:T(8,128)S(1)}, f32[1,128,1536]{2,1,0:T(8,128)}, u32[]{:S(2)}) copy-start(f32[1,128,1536]{2,1,0:T(8,128)} %param.8) | copy-start | bytes 2359300
  1.8 1.1 %copy-start.1 = (f32[1,128,1536]{2,1,0:T(8,128)S(1)}, f32[1,128,1536]{2,1,0:T(8,128)}, u32[]{:S(2)}) copy-start(f32[1,128,1536]{2,1,0:T(8,128)} %param.9) | copy-start | bytes 2359300
  2.9 1.1 %copy-start.2 = (f32[1,128,1536]{2,1,0:T(8,128)S(1)}, f32[1,128,1536]{2,1,0:T(8,128)}, u32[]{:S(2)}) copy-start(f32[1,128,1536]{2,1,0:T(8,128)} %param.10) | copy-start | bytes 2359300
  4.0 1.0 %copy-start.3 = (bf16[1,128,1536]{2,1,0:T(8,128)(2,1)S(1)}, bf16[1,128,1536]{2,1,0:T(8,128)(2,1)}, u32[]{:S(2)}) copy-start(bf16[1,128,1536]{2,1,0:T(8,128)(2,1)} %param.11) | copy-start | bytes 1179652
  5.0 0.7 copy-start.4
  5.7 0.7 copy-start.5

commit v3 on v2

--- a/solution.py
+++ b/solution.py
@@ -125,13 +125,17 @@
 
     gstep = gv.shape[0] // CHUNKS
     gone = [pl.ds(c * gstep, gstep) for c in range(CHUNKS)]
-    grad_four, grad_one = [], []
-
-    def send_gradient(c):
-        grad_four.append(ship(g_ref.at[gone[c]], gwin_ref.at[4, gone[c]], lower(4)))
-        grad_one.append(ship(g_ref.at[gone[c]], gwin_ref.at[1, gone[c]], lower(1)))
-
-    send_gradient(0)
+    grads = {1: [], 2: [], 3: [], 4: []}
+
+    def send_gradient(d, c):
+        grads[d].append(ship(g_ref.at[gone[c]], gwin_ref.at[d, gone[c]], lower(d)))
+
+    def relay_gradient(c):
+        grads[4][c].wait_recv()
+        grads[3].append(ship(gwin_ref.at[4, gone[c]], gwin_ref.at[3, gone[c]], higher(1)))
+
+    send_gradient(4, 0)
+    send_gradient(2, 0)
 
     lost_in.wait()
     blocks_in.wait()
@@ -165,19 +169,15 @@
     part_one[0] = lax.fori_loop(0, gv.shape[0] // step, add_rows, jnp.zeros((8, LANES), jnp.float32))
     ones = [ship(part_one.at[0], part_one.at[d], lower(d)) for d in range(1, 4)]
 
-    for c in range(1, CHUNKS):
-        send_gradient(c)
-
     for a in range(3):
         got[a][1].wait_recv()
         got[a][2] = ship(wins[a].at[1, :, left], wins[a].at[2, :, left], lower(1))
         got[a][3].wait_recv()
         got[a][5] = ship(wins[a].at[3, :, right], wins[a].at[2, :, right], higher(1))
 
-    for copy in ones:
-        copy.wait_recv()
-    part_two[0] = part_one[0] + part_one[1] + part_one[2] + part_one[3]
-    twos = [ship(part_two.at[0], part_two.at[k + 1], lower(d)) for k, d in enumerate(STAGE_TWO)]
+    send_gradient(4, 1)
+    send_gradient(1, 0)
+    send_gradient(2, 1)
 
     up, down, across = [], [], []
     for a in range(3):
@@ -191,13 +191,17 @@
         across.append(ship(sel.at[a], mine, to_partner, lands=gat_ref.at[a, :, piece(partner)]))
         kept.append(local(sel.at[a], mine))
 
-    grad_rest, grad_three = [], []
-    for c in range(CHUNKS):
-        grad_four[c].wait_recv()
-        grad_three.append(ship(gwin_ref.at[4, gone[c]], gwin_ref.at[3, gone[c]], higher(1)))
-        grad_one[c].wait_recv()
-        if c < CHUNKS // 2:
-            grad_rest.append(ship(gwin_ref.at[1, gone[c]], gwin_ref.at[2, gone[c]], lower(1)))
+    relay_gradient(0)
+    for c in range(2, CHUNKS):
+        send_gradient(4, c)
+        send_gradient(1, c - 1)
+        send_gradient(2, c)
+    send_gradient(1, CHUNKS - 1)
+
+    for copy in ones:
+        copy.wait_recv()
+    part_two[0] = part_one[0] + part_one[1] + part_one[2] + part_one[3]
+    twos = [ship(part_two.at[0], part_two.at[k + 1], lower(d)) for k, d in enumerate(STAGE_TWO)]
 
     partner_y = [lax.rem(partner + REP + 2 * dy, REP) for dy in range(4)]
 
@@ -207,6 +211,7 @@
 
     far = []
     for a in range(3):
+        relay_gradient(a + 1)
         up[a].wait_recv()
         theirs = gat_ref.at[a, :, piece(along_y(-1)), left]
         far.append(ship(theirs, theirs, chip_y(1), lands=gat_ref.at[a, :, piece(along_y(2)), left]))
@@ -215,10 +220,6 @@
         far.append(ship(theirs, theirs, chip_y(-1), lands=gat_ref.at[a, :, piece(along_y(2)), right]))
         cross(a, 3)
         cross(a, 1)
-    for c in range(CHUNKS):
-        grad_three[c].wait_recv()
-        if c >= CHUNKS // 2:
-            grad_rest.append(ship(gwin_ref.at[3, gone[c]], gwin_ref.at[2, gone[c]], higher(1)))
     for a in range(3):
         far[2 * a].wait_recv()
         far[2 * a + 1].wait_recv()
@@ -231,7 +232,7 @@
         total = total + part_two[k]
     norm_ref[...] = total
 
-    for copy in (*grad_rest, *across):
+    for copy in (*grads[1], *grads[2], *grads[3], *across):
         copy.wait_recv()
     for copy in sent:
         copy.wait_send()
@@ -298,7 +299,7 @@
             pltpu.SemaphoreType.DMA((72,)),
         ],
         compiler_params=pltpu.CompilerParams(
-            collective_id=0, has_side_effects=True, vmem_limit_bytes=24 * 2**20
+            collective_id=0, has_side_effects=True, vmem_limit_bytes=60 * 2**20
         ),
         name="gather_blocks",
     )(shard_lost, new_blocks, weights[0], first_moment[0], second_moment[0], gradient[0])
@@ -334,7 +335,7 @@
             out_specs=[out_spec] * 3,
             scratch_shapes=[pltpu.VMEM((8, 128), f32)],
         ),
-        compiler_params=pltpu.CompilerParams(vmem_limit_bytes=24 * 2**20),
+        compiler_params=pltpu.CompilerParams(vmem_limit_bytes=60 * 2**20),
         name="adam_update",
     )(meta, norm, gat, gwin)
     return tuple(out[None] for out in outs)

time: 76.1 us -> 61.1 us (0.80)
  the two profiles are of different devices: /device:TPU:8 before, /device:TPU:1 now
where the time goes in v3:
time: 61.1 us; the launch traced here: 60.9 us
  Pallas kernels  60.2 us (99%)
  between operations  0.64 us (1%)
    pallas_call x1, Pallas kernels, on_device(): pl.pallas_call(gather_kernel, out_shape=(jax.ShapeDtypeStruct((3, SLOTS,...  51.9 us
    pallas_call x1, Pallas kernels, on_device(): pl.pallas_call(functools.partial(update_kernel, limit), out_shape=[jax.Sh...  8.37 us

profile of v3, /device:TPU:1, one launch (start us, length us, event | category | flops | bytes accessed | tf_op | source)
XLA Modules:
  0.0 60.9 jit_solution(1924027308142598784)
XLA Ops:
  0.6 51.9 %gather_blocks.1 = (s16[3,3,128,1664]{3,2,1,0:T(8,128)(2,1)}, bf16[5,128,1536]{2,1,0:T(8,128)(2,1)}, f32[8,128]{1,0:T(8,128)}, s32[8]{0:T(128)}) custom-call(s32[8]{0:T(128)} %lost_hbm.1, s32[28]{0:T(128)} %blocks_hbm.1, f32[128,1536]{1,0:T(8,128)} %bitcast.7, f32[128,1536]{1,0:T(8,128)} %bitcast.8, f32[128,1536]{1,0:T(8,128)} %bitcast.9, ...), custom_call_target="tpu_custom_call" | custom-call | tf_op jit(solution)/shard_map/gather_blocks/pallas_call | solution.py:277
  52.5 8.4 %adam_update.1 = (f32[384,1536]{1,0:T(8,128)}, f32[384,1536]{1,0:T(8,128)}, f32[384,1536]{1,0:T(8,128)}) custom-call(s32[8]{0:T(128)} %get-tuple-element.10.meta_ref, f32[8,128]{1,0:T(8,128)} %get-tuple-element.11.norm_ref, s16[3,3,128,1664]{3,2,1,0:T(8,128)(2,1)} %get-tuple-element.12.gat_ref, bf16[5,128,1536]{2,1,0:T(8,128)(2,1)} %get-tuple-element.13.g_ref), custom_call_target="tpu_custom_call" | custom-call | tf_op jit(solution)/shard_map/adam_update/pallas_call | solution.py:324

commit v4 on v3

--- a/solution.py
+++ b/solution.py
@@ -18,12 +18,13 @@
 
 WIDE = 32
 REP = 8
+ROW = 4
 SHIFT = 4
 SLOTS = 3
 LANES = 128
 TOP = 32767.0
 CHUNKS = 4
-STAGE_TWO = tuple(range(4, WIDE, 4))
+STAGE_TWO = tuple(range(ROW, WIDE, ROW))
 MESH = pl.DeviceIdType.MESH
 
 
@@ -76,6 +77,11 @@
     def higher(d):
         return {"rep": island, "wide": lax.rem(shard + d, WIDE)}
 
+    column = lax.rem(shard, ROW)
+
+    def in_row(d):
+        return {"rep": island, "wide": shard - column + lax.rem(column + ROW - d, ROW)}
+
     def along_y(dy):
         return lax.rem(island + REP + 2 * dy, REP)
 
@@ -85,16 +91,16 @@
     def piece(p):
         return pl.ds(pl.multiple_of(p * rows, rows), rows)
 
-    def send(src, dst, where, lands=None):
+    def maker(where):
         k = used["remote"]
         used["remote"] = k + 1
-        copy = pltpu.make_async_remote_copy(src, dst, out_sem.at[k], in_sem.at[k], device_id=where, device_id_type=MESH)
-        copy.start()
-        if lands is None:
-            return copy, copy
-        return copy, pltpu.make_async_remote_copy(
-            src, lands, out_sem.at[k], in_sem.at[k], device_id=where, device_id_type=MESH
-        )
+
+        def make(src, dst):
+            return pltpu.make_async_remote_copy(
+                src, dst, out_sem.at[k], in_sem.at[k], device_id=where, device_id_type=MESH
+            )
+
+        return make
 
     def local(src, dst):
         k = used["local"]
@@ -105,18 +111,36 @@
 
     sent, kept = [], []
 
-    def ship(*args, **kwargs):
-        copy, lands = send(*args, **kwargs)
+    def ship(src, dst, where, lands=None):
+        make = maker(where)
+        copy = make(src, dst)
+        copy.start()
         sent.append(copy)
-        return lands
+        return copy if lands is None else make(src, lands)
+
+    def ship_in_row(d, own_src, above_src, dst):
+        make = maker(in_row(d))
+        copy = make(own_src, dst)
+        sent.append(copy)
+
+        @pl.when(column >= d)
+        def _():
+            copy.start()
+
+        def go():
+            @pl.when(column < d)
+            def _():
+                make(above_src, dst).start()
+
+        return copy, go
 
     grad_in = local(g_ref, gv)
     own_in = [local(arrays[a].at[piece(island)], own.at[a]) for a in range(3)]
     lost_in, blocks_in = local(lost_hbm, lost_ref), local(blocks_hbm, blocks_ref)
 
     barrier = pltpu.get_barrier_semaphore()
-    offsets = (1, 2, 3, *STAGE_TWO, WIDE - 1)
-    greeted = [*(higher(d) for d in offsets), chip_y(1), chip_y(-1), to_partner]
+    offsets = (1, *STAGE_TWO, WIDE - 1)
+    greeted = [*(higher(d) for d in offsets), *(in_row(d) for d in range(1, ROW)), chip_y(1), chip_y(-1), to_partner]
     for device in greeted:
         pl.semaphore_signal(barrier, inc=1, device_id=device, device_id_type=MESH)
     pl.semaphore_wait(barrier, len(greeted))
@@ -125,17 +149,28 @@
 
     gstep = gv.shape[0] // CHUNKS
     gone = [pl.ds(c * gstep, gstep) for c in range(CHUNKS)]
-    grads = {1: [], 2: [], 3: [], 4: []}
-
-    def send_gradient(d, c):
-        grads[d].append(ship(g_ref.at[gone[c]], gwin_ref.at[d, gone[c]], lower(d)))
-
-    def relay_gradient(c):
+    grads = {d: [None] * CHUNKS for d in range(1, SHIFT + 1)}
+    grad_go = [None] * CHUNKS
+
+    def grad_first(c):
+        rows_c = gone[c]
+        grads[4][c] = ship(g_ref.at[rows_c], gwin_ref.at[4, rows_c], lower(4))
+        grad_go[c] = []
+        for d in (1, 3):
+            grads[d][c], go = ship_in_row(d, g_ref.at[rows_c], gwin_ref.at[4, rows_c], gwin_ref.at[d, rows_c])
+            grad_go[c].append(go)
+
+    def grad_second(c):
         grads[4][c].wait_recv()
-        grads[3].append(ship(gwin_ref.at[4, gone[c]], gwin_ref.at[3, gone[c]], higher(1)))
-
-    send_gradient(4, 0)
-    send_gradient(2, 0)
+        for go in grad_go[c]:
+            go()
+
+    def grad_two(c, d):
+        grads[d][c].wait_recv()
+        to = lower(1) if d == 1 else higher(1)
+        grads[2][c] = ship(gwin_ref.at[d, gone[c]], gwin_ref.at[2, gone[c]], to)
+
+    grad_first(0)
 
     lost_in.wait()
     blocks_in.wait()
@@ -151,12 +186,63 @@
         meta_ref[1 + s] = gaps[s]
     broken = lost_ref[island] == shard
 
-    got = []
-    for a in range(3):
+    windows, ring, far, across = [], [], [], []
+
+    def code(a):
         own_in[a].wait()
         mend[a].wait_recv()
         encode(jnp.where(broken, fix[a], own[a]), wins[a].at[0])
-        got.append({d: ship(wins[a].at[0], wins[a].at[d], lower(d)) for d in (1, 3, 4)})
+
+    def first(a):
+        win = wins[a]
+        down = ship(win.at[0], win.at[4], lower(4))
+        windows.append((down, [ship_in_row(d, win.at[0], win.at[4], win.at[d]) for d in (2, 1, 3)]))
+
+    def second(a):
+        windows[a][0].wait_recv()
+        for _, go in windows[a][1]:
+            go()
+
+    def pick(a):
+        for lands, _ in windows[a][1]:
+            lands.wait_recv()
+        for s in range(SLOTS):
+            sel[a, s] = wins[a][gaps[s]]
+        mine = gat_ref.at[a, :, piece(island)]
+        ring.append(
+            (
+                ship(sel.at[a], mine, chip_y(1), lands=gat_ref.at[a, :, piece(along_y(-1))]),
+                ship(sel.at[a], mine, chip_y(-1), lands=gat_ref.at[a, :, piece(along_y(1))]),
+            )
+        )
+        across.append(ship(sel.at[a], mine, to_partner, lands=gat_ref.at[a, :, piece(partner)]))
+        kept.append(local(sel.at[a], mine))
+
+    def cross(a, dy):
+        theirs = gat_ref.at[a, :, piece(along_y(dy))]
+        lands = gat_ref.at[a, :, piece(lax.rem(partner + REP + 2 * dy, REP))]
+        across.append(ship(theirs, theirs, to_partner, lands=lands))
+
+    def pass_on(a):
+        halves = []
+        for copy, dy, half in ((ring[a][0], 1, left), (ring[a][1], -1, right)):
+            copy.wait_recv()
+            theirs = gat_ref.at[a, :, piece(along_y(-dy)), half]
+            halves.append(ship(theirs, theirs, chip_y(dy), lands=gat_ref.at[a, :, piece(along_y(2)), half]))
+            cross(a, -dy)
+        far.append(halves)
+
+    def close(a):
+        for copy in far[a]:
+            copy.wait_recv()
+        cross(a, 2)
+
+    code(0)
+    first(0)
+    code(1)
+    first(1)
+    code(2)
+    second(0)
 
     grad_in.wait()
     kept.append(local(gv, gwin_ref.at[0]))
@@ -167,63 +253,34 @@
         return total + fold(x * x)
 
     part_one[0] = lax.fori_loop(0, gv.shape[0] // step, add_rows, jnp.zeros((8, LANES), jnp.float32))
-    ones = [ship(part_one.at[0], part_one.at[d], lower(d)) for d in range(1, 4)]
-
-    for a in range(3):
-        got[a][1].wait_recv()
-        got[a][2] = ship(wins[a].at[1, :, left], wins[a].at[2, :, left], lower(1))
-        got[a][3].wait_recv()
-        got[a][5] = ship(wins[a].at[3, :, right], wins[a].at[2, :, right], higher(1))
-
-    send_gradient(4, 1)
-    send_gradient(1, 0)
-    send_gradient(2, 1)
-
-    up, down, across = [], [], []
-    for a in range(3):
-        for d in (4, 2, 5):
-            got[a][d].wait_recv()
-        for s in range(SLOTS):
-            sel[a, s] = wins[a][gaps[s]]
-        mine = gat_ref.at[a, :, piece(island)]
-        up.append(ship(sel.at[a], mine, chip_y(1), lands=gat_ref.at[a, :, piece(along_y(-1))]))
-        down.append(ship(sel.at[a], mine, chip_y(-1), lands=gat_ref.at[a, :, piece(along_y(1))]))
-        across.append(ship(sel.at[a], mine, to_partner, lands=gat_ref.at[a, :, piece(partner)]))
-        kept.append(local(sel.at[a], mine))
-
-    relay_gradient(0)
-    for c in range(2, CHUNKS):
-        send_gradient(4, c)
-        send_gradient(1, c - 1)
-        send_gradient(2, c)
-    send_gradient(1, CHUNKS - 1)
-
+    ones = [ship(part_one.at[0], part_one.at[d], in_row(d)) for d in range(1, ROW)]
+
+    pick(0)
+    first(2)
+    second(1)
+    for c in range(1, CHUNKS):
+        grad_first(c)
+    grad_second(0)
+    pick(1)
+    second(2)
     for copy in ones:
         copy.wait_recv()
     part_two[0] = part_one[0] + part_one[1] + part_one[2] + part_one[3]
     twos = [ship(part_two.at[0], part_two.at[k + 1], lower(d)) for k, d in enumerate(STAGE_TWO)]
-
-    partner_y = [lax.rem(partner + REP + 2 * dy, REP) for dy in range(4)]
-
-    def cross(a, dy):
-        theirs = gat_ref.at[a, :, piece(along_y(dy))]
-        across.append(ship(theirs, theirs, to_partner, lands=gat_ref.at[a, :, piece(partner_y[dy])]))
-
-    far = []
-    for a in range(3):
-        relay_gradient(a + 1)
-        up[a].wait_recv()
-        theirs = gat_ref.at[a, :, piece(along_y(-1)), left]
-        far.append(ship(theirs, theirs, chip_y(1), lands=gat_ref.at[a, :, piece(along_y(2)), left]))
-        down[a].wait_recv()
-        theirs = gat_ref.at[a, :, piece(along_y(1)), right]
-        far.append(ship(theirs, theirs, chip_y(-1), lands=gat_ref.at[a, :, piece(along_y(2)), right]))
-        cross(a, 3)
-        cross(a, 1)
-    for a in range(3):
-        far[2 * a].wait_recv()
-        far[2 * a + 1].wait_recv()
-        cross(a, 2)
+    grad_second(1)
+    grad_two(0, 3)
+    pick(2)
+    grad_second(2)
+    grad_two(2, 1)
+    pass_on(0)
+    grad_two(1, 3)
+    grad_second(3)
+    pass_on(1)
+    grad_two(3, 1)
+    pass_on(2)
+    close(0)
+    close(1)
+    close(2)
 
     for copy in twos:
         copy.wait_recv()
@@ -232,7 +289,7 @@
         total = total + part_two[k]
     norm_ref[...] = total
 
-    for copy in (*grads[1], *grads[2], *grads[3], *across):
+    for copy in (*grads[1][:2], *grads[2], *grads[3][2:], *across):
         copy.wait_recv()
     for copy in sent:
         copy.wait_send()

time: 61.1 us -> 52.9 us (0.87)
  the two profiles are of different devices: /device:TPU:1 before, /device:TPU:7 now
where the time goes in v4:
time: 52.9 us; the launch traced here: 52.7 us
  Pallas kernels  52 us (98%)
  between operations  0.64 us (1%)
    pallas_call x1, Pallas kernels, on_device(): pl.pallas_call(gather_kernel, out_shape=(jax.ShapeDtypeStruct((3, SLOTS,...  45.1 us
    pallas_call x1, Pallas kernels, on_device(): pl.pallas_call(functools.partial(update_kernel, limit), out_shape=[jax.Sh...  6.94 us

profile of v4, /device:TPU:7, one launch (start us, length us, event | category | flops | bytes accessed | tf_op | source)
XLA Modules:
  0.0 52.7 jit_solution(8435453385506331767)
XLA Ops:
  0.6 45.1 %gather_blocks.1 = (s16[3,3,128,1664]{3,2,1,0:T(8,128)(2,1)}, bf16[5,128,1536]{2,1,0:T(8,128)(2,1)}, f32[8,128]{1,0:T(8,128)}, s32[8]{0:T(128)}) custom-call(s32[8]{0:T(128)} %lost_hbm.1, s32[28]{0:T(128)} %blocks_hbm.1, f32[128,1536]{1,0:T(8,128)} %bitcast.7, f32[128,1536]{1,0:T(8,128)} %bitcast.8, f32[128,1536]{1,0:T(8,128)} %bitcast.9, ...), custom_call_target="tpu_custom_call" | custom-call | tf_op jit(solution)/shard_map/gather_blocks/pallas_call | solution.py:334
  45.7 6.9 %adam_update.1 = (f32[384,1536]{1,0:T(8,128)}, f32[384,1536]{1,0:T(8,128)}, f32[384,1536]{1,0:T(8,128)}) custom-call(s32[8]{0:T(128)} %get-tuple-element.10.meta_ref, f32[8,128]{1,0:T(8,128)} %get-tuple-element.11.norm_ref, s16[3,3,128,1664]{3,2,1,0:T(8,128)(2,1)} %get-tuple-element.12.gat_ref, bf16[5,128,1536]{2,1,0:T(8,128)(2,1)} %get-tuple-element.13.g_ref), custom_call_target="tpu_custom_call" | custom-call | tf_op jit(solution)/shard_map/adam_update/pallas_call | solution.py:381

commit v5 on v4

--- a/solution.py
+++ b/solution.py
@@ -24,6 +24,7 @@
 LANES = 128
 TOP = 32767.0
 CHUNKS = 4
+STEP = 32
 STAGE_TWO = tuple(range(ROW, WIDE, ROW))
 MESH = pl.DeviceIdType.MESH
 
@@ -39,10 +40,10 @@
     out[:, x.shape[1] :] = tail.astype(jnp.int32).astype(jnp.int16)
 
 
-def decode(x):
+def decode(x, times):
     columns = x.shape[1] - LANES
     code = x[:, :columns].astype(jnp.int32).astype(jnp.float32)
-    scale = jnp.exp2(x[:, columns:].astype(jnp.int32).astype(jnp.float32)) * (1.0 / TOP**2)
+    scale = jnp.exp2(x[:, columns:].astype(jnp.int32).astype(jnp.float32)) * (times / TOP**2)
     return code * jnp.abs(code) * jnp.concatenate([scale] * (columns // LANES), axis=1)
 
 
@@ -258,26 +259,26 @@
     pick(0)
     first(2)
     second(1)
-    for c in range(1, CHUNKS):
-        grad_first(c)
     grad_second(0)
     pick(1)
     second(2)
+    for c in range(1, CHUNKS):
+        grad_first(c)
     for copy in ones:
         copy.wait_recv()
     part_two[0] = part_one[0] + part_one[1] + part_one[2] + part_one[3]
     twos = [ship(part_two.at[0], part_two.at[k + 1], lower(d)) for k, d in enumerate(STAGE_TWO)]
-    grad_second(1)
     grad_two(0, 3)
     pick(2)
+    grad_second(1)
+    pass_on(0)
     grad_second(2)
-    grad_two(2, 1)
-    pass_on(0)
     grad_two(1, 3)
+    pass_on(1)
     grad_second(3)
-    pass_on(1)
+    grad_two(2, 3)
+    pass_on(2)
     grad_two(3, 1)
-    pass_on(2)
     close(0)
     close(1)
     close(2)
@@ -289,7 +290,7 @@
         total = total + part_two[k]
     norm_ref[...] = total
 
-    for copy in (*grads[1][:2], *grads[2], *grads[3][2:], *across):
+    for copy in (grads[1][0], grads[1][1], grads[1][2], grads[3][3], *grads[2], *across):
         copy.wait_recv()
     for copy in sent:
         copy.wait_send()
@@ -297,30 +298,82 @@
         copy.wait()
 
 
-def update_kernel(limit, meta_ref, norm_ref, gat_ref, g_ref, w_out, m_out, v_out, factor_ref):
-    slot, part = pl.program_id(0), pl.program_id(1)
-
-    @pl.when(jnp.logical_and(slot == 0, part == 0))
-    def _():
-        norm_sum = jnp.sum(norm_ref[...], keepdims=True)
-        factor_ref[...] = jnp.broadcast_to(jnp.minimum(1.0, limit / (jnp.sqrt(norm_sum) + 1e-06)), factor_ref.shape)
-
-    @pl.when(slot < meta_ref[0])
-    def _():
-        factor = factor_ref[0:1, 0:1]
-        params, moment_one, moment_two = (decode(gat_ref[a, 0]) for a in range(3))
-        clipped = g_ref[0].astype(jnp.float32) * factor
-        one_new = beta_first * moment_one + (1.0 - beta_first) * clipped
-        two_new = beta_second * moment_two + (1.0 - beta_second) * clipped * clipped
-        step_dir = one_new / bias_first / (jnp.sqrt(two_new / bias_second) + eps_adam)
-        w_out[...] = params - learn_rate * (step_dir + weight_decay * params)
-        m_out[...] = one_new
-        v_out[...] = two_new
-
-    @pl.when(slot >= meta_ref[0])
-    def _():
-        for out in (w_out, m_out, v_out):
-            out[...] = jnp.zeros_like(out)
+def update_kernel(
+    limit, meta_ref, norm_ref, gat_ref, gwin_ref, w_out, m_out, v_out,
+    codes, grads, fresh, zeros, in_sem, grad_sem, out_sem, zero_sem,
+):
+    outs = (w_out, m_out, v_out)
+    block = codes.shape[2]
+    steps = block // STEP
+    count = meta_ref[0]
+
+    def fetch(s):
+        copies = [pltpu.make_async_copy(gat_ref.at[a, s], codes.at[a, s], in_sem.at[a, s]) for a in range(3)]
+        return (*copies, pltpu.make_async_copy(gwin_ref.at[meta_ref[1 + s]], grads.at[s], grad_sem.at[s]))
+
+    def clear(s):
+        return [pltpu.make_async_copy(zeros, outs[a].at[pl.ds(s * block, block)], zero_sem.at[a, s]) for a in range(3)]
+
+    def give(a, s, i):
+        rows = pl.ds(pl.multiple_of(i * STEP, STEP), STEP)
+        there = pl.ds(pl.multiple_of(s * block + i * STEP, STEP), STEP)
+        return pltpu.make_async_copy(fresh.at[a, s, rows], outs[a].at[there], out_sem.at[a, s, i])
+
+    for s in range(SLOTS):
+
+        @pl.when(s < count)
+        def _(s=s):
+            for copy in fetch(s):
+                copy.start()
+
+    zeros[...] = jnp.zeros_like(zeros)
+    for s in range(SLOTS):
+
+        @pl.when(s >= count)
+        def _(s=s):
+            for copy in clear(s):
+                copy.start()
+
+    norm_sum = jnp.sum(norm_ref[...], keepdims=True)
+    factor = jnp.minimum(1.0, limit / (jnp.sqrt(norm_sum) + 1e-06))
+    share_one = (1.0 - beta_first) * factor
+    share_two = (1.0 - beta_second) * factor * factor
+
+    for s in range(SLOTS):
+
+        @pl.when(s < count)
+        def _(s=s):
+            for copy in fetch(s):
+                copy.wait()
+
+            def some_rows(i, carry):
+                rows = pl.ds(pl.multiple_of(i * STEP, STEP), STEP)
+                grad = grads[s, rows].astype(jnp.float32)
+                one_new = decode(codes[1, s, rows], beta_first) + grad * share_one
+                two_new = decode(codes[2, s, rows], beta_second) + grad * grad * share_two
+                scaled = two_new * (1.0 / bias_second)
+                step_dir = one_new * (learn_rate / bias_first) / (scaled * lax.rsqrt(scaled) + eps_adam)
+                fresh[0, s, rows] = decode(codes[0, s, rows], 1.0 - learn_rate * weight_decay) - step_dir
+                fresh[1, s, rows] = one_new
+                fresh[2, s, rows] = two_new
+                for a in range(3):
+                    give(a, s, i).start()
+                return carry
+
+            lax.fori_loop(0, steps, some_rows, 0)
+
+    for s in range(SLOTS):
+
+        @pl.when(s < count)
+        def _(s=s):
+            for a in range(3):
+                for i in range(steps):
+                    give(a, s, i).wait()
+
+        @pl.when(s >= count)
+        def _(s=s):
+            for copy in clear(s):
+                copy.wait()
 
 
 def on_device(shard_lost, new_blocks, weights, first_moment, second_moment, gradient):
@@ -361,37 +414,22 @@
         name="gather_blocks",
     )(shard_lost, new_blocks, weights[0], first_moment[0], second_moment[0], gradient[0])
 
-    chunk = 64
-    parts = block // chunk
-
-    def source(slot, part, meta_ref):
-        last = jnp.maximum(meta_ref[0], 1) - 1
-        return jnp.minimum(slot, last), jnp.where(slot > last, parts - 1, part)
-
-    def gat_map(slot, part, meta_ref):
-        s, i = source(slot, part, meta_ref)
-        return 0, s, i, 0
-
-    def grad_map(slot, part, meta_ref):
-        s, i = source(slot, part, meta_ref)
-        return meta_ref[1 + s], i, 0
-
-    out_spec = pl.BlockSpec((chunk, ff), lambda slot, part, meta_ref: (slot * parts + part, 0))
     limit = 0.5 * math.sqrt(block * WIDE * ff)
     outs = pl.pallas_call(
         functools.partial(update_kernel, limit),
         out_shape=[jax.ShapeDtypeStruct((SLOTS * block, ff), f32)] * 3,
-        grid_spec=pltpu.PrefetchScalarGridSpec(
-            num_scalar_prefetch=1,
-            grid=(SLOTS, parts),
-            in_specs=[
-                pl.BlockSpec((8, 128), lambda slot, part, meta_ref: (0, 0)),
-                pl.BlockSpec((3, 1, chunk, width), gat_map),
-                pl.BlockSpec((1, chunk, ff), grad_map),
-            ],
-            out_specs=[out_spec] * 3,
-            scratch_shapes=[pltpu.VMEM((8, 128), f32)],
-        ),
+        in_specs=[smem, vmem, anywhere, anywhere],
+        out_specs=[anywhere] * 3,
+        scratch_shapes=[
+            pltpu.VMEM((3, SLOTS, block, width), jnp.int16),
+            pltpu.VMEM((SLOTS, block, ff), jnp.bfloat16),
+            pltpu.VMEM((3, SLOTS, block, ff), f32),
+            pltpu.VMEM((block, ff), f32),
+            pltpu.SemaphoreType.DMA((3, SLOTS)),
+            pltpu.SemaphoreType.DMA((SLOTS,)),
+            pltpu.SemaphoreType.DMA((3, SLOTS, block // STEP)),
+            pltpu.SemaphoreType.DMA((3, SLOTS)),
+        ],
         compiler_params=pltpu.CompilerParams(vmem_limit_bytes=60 * 2**20),
         name="adam_update",
     )(meta, norm, gat, gwin)

time: 52.9 us -> 47.9 us (0.905)
  the two profiles are of different devices: /device:TPU:7 before, /device:TPU:1 now
where the time goes in v5:
time: 47.9 us; the launch traced here: 47 us
  Pallas kernels  46.4 us (97%)
  between operations  0.64 us (1%)
    pallas_call x1, Pallas kernels, on_device(): pl.pallas_call(gather_kernel, out_shape=(jax.ShapeDtypeStruct((3, SLOTS,...  40.1 us
    pallas_call x1, Pallas kernels, on_device(): pl.pallas_call(functools.partial(update_kernel, limit), out_shape=[jax.Sh...  6.27 us

profile of v5, /device:TPU:1, one launch (start us, length us, event | category | flops | bytes accessed | tf_op | source)
XLA Modules:
  0.0 47.0 jit_solution(9018004466873553337)
XLA Ops:
  0.6 40.1 %gather_blocks.1 = (s16[3,3,128,1664]{3,2,1,0:T(8,128)(2,1)}, bf16[5,128,1536]{2,1,0:T(8,128)(2,1)}, f32[8,128]{1,0:T(8,128)}, s32[8]{0:T(128)}) custom-call(s32[8]{0:T(128)} %lost_hbm.1, s32[28]{0:T(128)} %blocks_hbm.1, f32[128,1536]{1,0:T(8,128)} %bitcast.7, f32[128,1536]{1,0:T(8,128)} %bitcast.8, f32[128,1536]{1,0:T(8,128)} %bitcast.9, ...), custom_call_target="tpu_custom_call" | custom-call | tf_op jit(solution)/shard_map/gather_blocks/pallas_call | solution.py:387
  40.7 6.3 %adam_update.1 = (f32[384,1536]{1,0:T(8,128)}, f32[384,1536]{1,0:T(8,128)}, f32[384,1536]{1,0:T(8,128)}) custom-call(s32[8]{0:T(128)} %get-tuple-element.10.meta_ref, f32[8,128]{1,0:T(8,128)} %get-tuple-element.11.norm_ref, s16[3,3,128,1664]{3,2,1,0:T(8,128)(2,1)} %get-tuple-element.12.gat_ref, bf16[5,128,1536]{2,1,0:T(8,128)(2,1)} %get-tuple-element.13.gwin_ref), custom_call_target="tpu_custom_call" | custom-call | tf_op jit(solution)/shard_map/adam_update/pallas_call | solution.py:418

commit v6 on v5

--- a/solution.py
+++ b/solution.py
@@ -238,30 +238,29 @@
             copy.wait_recv()
         cross(a, 2)
 
+    grad_in.wait()
+    kept.append(local(gv, gwin_ref.at[0]))
+    step = 16
+
+    def add_rows(i, total):
+        x = gv[pl.ds(pl.multiple_of(i * step, step), step), :].astype(jnp.float32)
+        return total + fold(x * x)
+
+    part_one[0] = lax.fori_loop(0, gv.shape[0] // step, add_rows, jnp.zeros((8, LANES), jnp.float32))
+    ones = [ship(part_one.at[0], part_one.at[d], in_row(d)) for d in range(1, ROW)]
+
     code(0)
     first(0)
     code(1)
     first(1)
     code(2)
+    first(2)
     second(0)
-
-    grad_in.wait()
-    kept.append(local(gv, gwin_ref.at[0]))
-    step = 16
-
-    def add_rows(i, total):
-        x = gv[pl.ds(pl.multiple_of(i * step, step), step), :].astype(jnp.float32)
-        return total + fold(x * x)
-
-    part_one[0] = lax.fori_loop(0, gv.shape[0] // step, add_rows, jnp.zeros((8, LANES), jnp.float32))
-    ones = [ship(part_one.at[0], part_one.at[d], in_row(d)) for d in range(1, ROW)]
-
+    second(1)
+    second(2)
     pick(0)
-    first(2)
-    second(1)
     grad_second(0)
     pick(1)
-    second(2)
     for c in range(1, CHUNKS):
         grad_first(c)
     for copy in ones:

time: 47.9 us -> 48.4 us (1.010); the launches traced: 47 us -> 48.3 us
  Pallas kernels: 46.4 us -> 47.7 us
    pallas_call x1, Pallas kernels: 40.1 us -> 41.4 us  [on_device(): pl.pallas_call(gather_kernel, out_shape=(jax.ShapeDtypeStruct((3, SLOTS,...]
where the time goes in v6:
time: 48.4 us; the launch traced here: 48.3 us
  Pallas kernels  47.7 us (99%)
  between operations  0.64 us (1%)
    pallas_call x1, Pallas kernels, on_device(): pl.pallas_call(gather_kernel, out_shape=(jax.ShapeDtypeStruct((3, SLOTS,...  41.4 us
    pallas_call x1, Pallas kernels, on_device(): pl.pallas_call(functools.partial(update_kernel, limit), out_shape=[jax.Sh...  6.27 us

profile of v6, /device:TPU:1, one launch (start us, length us, event | category | flops | bytes accessed | tf_op | source)
XLA Modules:
  0.0 48.3 jit_solution(17682527152340610931)
XLA Ops:
  0.6 41.4 %gather_blocks.1 = (s16[3,3,128,1664]{3,2,1,0:T(8,128)(2,1)}, bf16[5,128,1536]{2,1,0:T(8,128)(2,1)}, f32[8,128]{1,0:T(8,128)}, s32[8]{0:T(128)}) custom-call(s32[8]{0:T(128)} %lost_hbm.1, s32[28]{0:T(128)} %blocks_hbm.1, f32[128,1536]{1,0:T(8,128)} %bitcast.7, f32[128,1536]{1,0:T(8,128)} %bitcast.8, f32[128,1536]{1,0:T(8,128)} %bitcast.9, ...), custom_call_target="tpu_custom_call" | custom-call | tf_op jit(solution)/shard_map/gather_blocks/pallas_call | solution.py:386
  42.0 6.3 %adam_update.1 = (f32[384,1536]{1,0:T(8,128)}, f32[384,1536]{1,0:T(8,128)}, f32[384,1536]{1,0:T(8,128)}) custom-call(s32[8]{0:T(128)} %get-tuple-element.10.meta_ref, f32[8,128]{1,0:T(8,128)} %get-tuple-element.11.norm_ref, s16[3,3,128,1664]{3,2,1,0:T(8,128)(2,1)} %get-tuple-element.12.gat_ref, bf16[5,128,1536]{2,1,0:T(8,128)(2,1)} %get-tuple-element.13.gwin_ref), custom_call_target="tpu_custom_call" | custom-call | tf_op jit(solution)/shard_map/adam_update/pallas_call | solution.py:417

commit v7 on v6

--- a/solution.py
+++ b/solution.py
@@ -29,22 +29,23 @@
 MESH = pl.DeviceIdType.MESH
 
 
+def lanes_of(width):
+    return (width - LANES, width - LANES, width)
+
+
 def encode(x, out):
     size = jnp.abs(x)
     most = jnp.clip(jnp.max(size, axis=1, keepdims=True), 2.0**-120, 2.0**120)
     exponent = jnp.ceil(jnp.log2(most))
     code = jnp.minimum(jnp.round(jnp.sqrt(size * jnp.exp2(-exponent)) * TOP), TOP)
-    code = jnp.where(x < 0, -code, code)
-    out[:, : x.shape[1]] = code.astype(jnp.int32).astype(jnp.int16)
-    tail = jnp.broadcast_to(exponent, (x.shape[0], LANES))
-    out[:, x.shape[1] :] = tail.astype(jnp.int32).astype(jnp.int16)
-
-
-def decode(x, times):
-    columns = x.shape[1] - LANES
-    code = x[:, :columns].astype(jnp.int32).astype(jnp.float32)
-    scale = jnp.exp2(x[:, columns:].astype(jnp.int32).astype(jnp.float32)) * (times / TOP**2)
-    return code * jnp.abs(code) * jnp.concatenate([scale] * (columns // LANES), axis=1)
+    out[:, : x.shape[1]] = jnp.where(x < 0, -code, code).astype(jnp.int32).astype(jnp.int16)
+    return jnp.broadcast_to(exponent, (x.shape[0], LANES))
+
+
+def decode(x, scale, times):
+    code = x.astype(jnp.int32).astype(jnp.float32)
+    scale = jnp.broadcast_to(scale * (times / TOP**2), (x.shape[0], LANES))
+    return code * jnp.abs(code) * jnp.concatenate([scale] * (x.shape[1] // LANES), axis=1)
 
 
 def fold(squares):
@@ -58,17 +59,15 @@
 def gather_kernel(
     lost_hbm, blocks_hbm, w_ref, m_ref, v_ref, g_ref,
     gat_ref, gwin_ref, norm_ref, meta_ref,
-    lost_ref, blocks_ref, own, fix, win_w, win_m, win_v, sel, gv, part_one, part_two, loc, out_sem, in_sem,
+    lost_ref, blocks_ref, own, fix, gv, part_one, part_two, loc, out_sem, in_sem, *buffers,
 ):
     arrays = (w_ref, m_ref, v_ref)
-    wins = (win_w, win_m, win_v)
+    units = lanes_of(gat_ref.shape[3])
+    wins, sels = buffers[:3], buffers[3:]
     rows = own.shape[1]
     island = lax.axis_index("rep")
     shard = lax.axis_index("wide")
     partner = island + 1 - 2 * lax.rem(island, 2)
-    width = sel.shape[3]
-    middle = width // LANES // 2 * LANES
-    left, right = pl.ds(0, middle), pl.ds(middle, width - middle)
     to_partner = {"rep": partner, "wide": shard}
     used = {"remote": 0, "local": 0}
 
@@ -189,54 +188,66 @@
 
     windows, ring, far, across = [], [], [], []
 
+    tails = []
+
     def code(a):
         own_in[a].wait()
         mend[a].wait_recv()
-        encode(jnp.where(broken, fix[a], own[a]), wins[a].at[0])
-
-    def first(a):
-        win = wins[a]
+        tails.append(encode(jnp.where(broken, fix[a], own[a]), wins[a].at[0]))
+        if a == 2:
+            lane = lax.broadcasted_iota(jnp.int32, tails[0].shape, 1)
+            tail = jnp.where(lane == 0, tails[0], jnp.where(lane == 1, tails[1], tails[2]))
+            wins[2][0, :, units[1] :] = tail.astype(jnp.int32).astype(jnp.int16)
+
+    def first(u):
+        win = wins[u]
         down = ship(win.at[0], win.at[4], lower(4))
         windows.append((down, [ship_in_row(d, win.at[0], win.at[4], win.at[d]) for d in (2, 1, 3)]))
 
-    def second(a):
-        windows[a][0].wait_recv()
-        for _, go in windows[a][1]:
+    def second(u):
+        windows[u][0].wait_recv()
+        for _, go in windows[u][1]:
             go()
 
-    def pick(a):
-        for lands, _ in windows[a][1]:
+    def slot(u, p, half=None):
+        start, lanes = 0, units[u]
+        middle = lanes // LANES // 2 * LANES
+        if half is not None:
+            start, lanes = (start, middle) if half == 0 else (start + middle, lanes - middle)
+        return gat_ref.at[u, :, piece(p), pl.ds(start, lanes)]
+
+    def pick(u):
+        for lands, _ in windows[u][1]:
             lands.wait_recv()
         for s in range(SLOTS):
-            sel[a, s] = wins[a][gaps[s]]
-        mine = gat_ref.at[a, :, piece(island)]
+            sels[u][s] = wins[u][gaps[s]]
+        mine = slot(u, island)
         ring.append(
             (
-                ship(sel.at[a], mine, chip_y(1), lands=gat_ref.at[a, :, piece(along_y(-1))]),
-                ship(sel.at[a], mine, chip_y(-1), lands=gat_ref.at[a, :, piece(along_y(1))]),
+                ship(sels[u], mine, chip_y(1), lands=slot(u, along_y(-1))),
+                ship(sels[u], mine, chip_y(-1), lands=slot(u, along_y(1))),
             )
         )
-        across.append(ship(sel.at[a], mine, to_partner, lands=gat_ref.at[a, :, piece(partner)]))
-        kept.append(local(sel.at[a], mine))
-
-    def cross(a, dy):
-        theirs = gat_ref.at[a, :, piece(along_y(dy))]
-        lands = gat_ref.at[a, :, piece(lax.rem(partner + REP + 2 * dy, REP))]
-        across.append(ship(theirs, theirs, to_partner, lands=lands))
-
-    def pass_on(a):
+        across.append(ship(sels[u], mine, to_partner, lands=slot(u, partner)))
+        kept.append(local(sels[u], mine))
+
+    def cross(u, dy):
+        theirs = slot(u, along_y(dy))
+        across.append(ship(theirs, theirs, to_partner, lands=slot(u, lax.rem(partner + REP + 2 * dy, REP))))
+
+    def pass_on(u):
         halves = []
-        for copy, dy, half in ((ring[a][0], 1, left), (ring[a][1], -1, right)):
+        for half, dy in enumerate((1, -1)):
+            ring[u][half].wait_recv()
+            theirs = slot(u, along_y(-dy), half)
+            halves.append(ship(theirs, theirs, chip_y(dy), lands=slot(u, along_y(2), half)))
+            cross(u, -dy)
+        far.append(halves)
+
+    def close(u):
+        for copy in far[u]:
             copy.wait_recv()
-            theirs = gat_ref.at[a, :, piece(along_y(-dy)), half]
-            halves.append(ship(theirs, theirs, chip_y(dy), lands=gat_ref.at[a, :, piece(along_y(2)), half]))
-            cross(a, -dy)
-        far.append(halves)
-
-    def close(a):
-        for copy in far[a]:
-            copy.wait_recv()
-        cross(a, 2)
+        cross(u, 2)
 
     grad_in.wait()
     kept.append(local(gv, gwin_ref.at[0]))
@@ -305,9 +316,15 @@
     block = codes.shape[2]
     steps = block // STEP
     count = meta_ref[0]
+    columns = fresh.shape[3]
 
     def fetch(s):
-        copies = [pltpu.make_async_copy(gat_ref.at[a, s], codes.at[a, s], in_sem.at[a, s]) for a in range(3)]
+        copies = []
+        for a, lanes in enumerate(lanes_of(codes.shape[3])):
+            part = pl.ds(0, lanes)
+            copies.append(
+                pltpu.make_async_copy(gat_ref.at[a, s, :, part], codes.at[a, s, :, part], in_sem.at[a, s])
+            )
         return (*copies, pltpu.make_async_copy(gwin_ref.at[meta_ref[1 + s]], grads.at[s], grad_sem.at[s]))
 
     def clear(s):
@@ -348,11 +365,12 @@
             def some_rows(i, carry):
                 rows = pl.ds(pl.multiple_of(i * STEP, STEP), STEP)
                 grad = grads[s, rows].astype(jnp.float32)
-                one_new = decode(codes[1, s, rows], beta_first) + grad * share_one
-                two_new = decode(codes[2, s, rows], beta_second) + grad * grad * share_two
+                scale = jnp.exp2(codes[2, s, rows, columns:].astype(jnp.int32).astype(jnp.float32))
+                one_new = decode(codes[1, s, rows, :columns], scale[:, 1:2], beta_first) + grad * share_one
+                two_new = decode(codes[2, s, rows, :columns], scale[:, 2:3], beta_second) + grad * grad * share_two
                 scaled = two_new * (1.0 / bias_second)
                 step_dir = one_new * (learn_rate / bias_first) / (scaled * lax.rsqrt(scaled) + eps_adam)
-                fresh[0, s, rows] = decode(codes[0, s, rows], 1.0 - learn_rate * weight_decay) - step_dir
+                fresh[0, s, rows] = decode(codes[0, s, rows, :columns], scale[:, 0:1], 1.0 - learn_rate * weight_decay) - step_dir
                 fresh[1, s, rows] = one_new
                 fresh[2, s, rows] = two_new
                 for a in range(3):
@@ -398,14 +416,14 @@
             pltpu.SMEM(new_blocks.shape, jnp.int32),
             pltpu.VMEM((3, rows, ff), f32),
             pltpu.VMEM((3, rows, ff), f32),
-            *[pltpu.VMEM((SHIFT + 1, rows, width), jnp.int16)] * 3,
-            pltpu.VMEM((3, SLOTS, rows, width), jnp.int16),
             pltpu.VMEM((block, ff), jnp.bfloat16),
             pltpu.VMEM((4, 8, LANES), f32),
             pltpu.VMEM((8, 8, LANES), f32),
-            pltpu.SemaphoreType.DMA((10,)),
-            pltpu.SemaphoreType.DMA((72,)),
-            pltpu.SemaphoreType.DMA((72,)),
+            pltpu.SemaphoreType.DMA((12,)),
+            pltpu.SemaphoreType.DMA((104,)),
+            pltpu.SemaphoreType.DMA((104,)),
+            *[pltpu.VMEM((SHIFT + 1, rows, lanes), jnp.int16) for lanes in lanes_of(width)],
+            *[pltpu.VMEM((SLOTS, rows, lanes), jnp.int16) for lanes in lanes_of(width)],
         ],
         compiler_params=pltpu.CompilerParams(
             collective_id=0, has_side_effects=True, vmem_limit_bytes=60 * 2**20

time: 48.4 us -> 48.7 us (level)
  no operation moved by 1% of the time
where the time goes in v7:
time: 48.7 us; the launch traced here: 48.4 us
  Pallas kernels  47.8 us (98%)
  between operations  0.64 us (1%)
    pallas_call x1, Pallas kernels, on_device(): pl.pallas_call(gather_kernel, out_shape=(jax.ShapeDtypeStruct((3, SLOTS,...  41.4 us
    pallas_call x1, Pallas kernels, on_device(): pl.pallas_call(functools.partial(update_kernel, limit), out_shape=[jax.Sh...  6.37 us

profile of v7, /device:TPU:1, one launch (start us, length us, event | category | flops | bytes accessed | tf_op | source)
XLA Modules:
  0.0 48.4 jit_solution(16100480192619399854)
XLA Ops:
  0.6 41.4 %gather_blocks.1 = (s16[3,3,128,1664]{3,2,1,0:T(8,128)(2,1)}, bf16[5,128,1536]{2,1,0:T(8,128)(2,1)}, f32[8,128]{1,0:T(8,128)}, s32[8]{0:T(128)}) custom-call(s32[8]{0:T(128)} %lost_hbm.1, s32[28]{0:T(128)} %blocks_hbm.1, f32[128,1536]{1,0:T(8,128)} %bitcast.7, f32[128,1536]{1,0:T(8,128)} %bitcast.8, f32[128,1536]{1,0:T(8,128)} %bitcast.9, ...), custom_call_target="tpu_custom_call" | custom-call | tf_op jit(solution)/shard_map/gather_blocks/pallas_call | solution.py:404
  42.0 6.4 %adam_update.1 = (f32[384,1536]{1,0:T(8,128)}, f32[384,1536]{1,0:T(8,128)}, f32[384,1536]{1,0:T(8,128)}) custom-call(s32[8]{0:T(128)} %get-tuple-element.10.meta_ref, f32[8,128]{1,0:T(8,128)} %get-tuple-element.11.norm_ref, s16[3,3,128,1664]{3,2,1,0:T(8,128)(2,1)} %get-tuple-element.12.gat_ref, bf16[5,128,1536]{2,1,0:T(8,128)(2,1)} %get-tuple-element.13.gwin_ref), custom_call_target="tpu_custom_call" | custom-call | tf_op jit(solution)/shard_map/adam_update/pallas_call | solution.py:435

commit v8 on v5

--- a/solution.py
+++ b/solution.py
@@ -40,11 +40,9 @@
     out[:, x.shape[1] :] = tail.astype(jnp.int32).astype(jnp.int16)
 
 
-def decode(x, times):
-    columns = x.shape[1] - LANES
-    code = x[:, :columns].astype(jnp.int32).astype(jnp.float32)
-    scale = jnp.exp2(x[:, columns:].astype(jnp.int32).astype(jnp.float32)) * (times / TOP**2)
-    return code * jnp.abs(code) * jnp.concatenate([scale] * (columns // LANES), axis=1)
+def decode(x, scale):
+    code = x.astype(jnp.int32).astype(jnp.float32)
+    return code * jnp.abs(code) * scale
 
 
 def fold(squares):
@@ -306,6 +304,7 @@
     block = codes.shape[2]
     steps = block // STEP
     count = meta_ref[0]
+    columns = fresh.shape[3]
 
     def fetch(s):
         copies = [pltpu.make_async_copy(gat_ref.at[a, s], codes.at[a, s], in_sem.at[a, s]) for a in range(3)]
@@ -348,14 +347,22 @@
 
             def some_rows(i, carry):
                 rows = pl.ds(pl.multiple_of(i * STEP, STEP), STEP)
-                grad = grads[s, rows].astype(jnp.float32)
-                one_new = decode(codes[1, s, rows], beta_first) + grad * share_one
-                two_new = decode(codes[2, s, rows], beta_second) + grad * grad * share_two
-                scaled = two_new * (1.0 / bias_second)
-                step_dir = one_new * (learn_rate / bias_first) / (scaled * lax.rsqrt(scaled) + eps_adam)
-                fresh[0, s, rows] = decode(codes[0, s, rows], 1.0 - learn_rate * weight_decay) - step_dir
-                fresh[1, s, rows] = one_new
-                fresh[2, s, rows] = two_new
+                times = (1.0 - learn_rate * weight_decay, beta_first, beta_second)
+                scales = [
+                    jnp.exp2(codes[a, s, rows, columns:].astype(jnp.int32).astype(jnp.float32)) * (times[a] / TOP**2)
+                    for a in range(3)
+                ]
+                for start in range(0, columns, LANES):
+                    part = pl.ds(start, LANES)
+                    params, moment_one, moment_two = (decode(codes[a, s, rows, part], scales[a]) for a in range(3))
+                    grad = grads[s, rows, part].astype(jnp.float32)
+                    one_new = moment_one + grad * share_one
+                    two_new = moment_two + grad * grad * share_two
+                    scaled = two_new * (1.0 / bias_second)
+                    step_dir = one_new * (learn_rate / bias_first) / (scaled * lax.rsqrt(scaled) + eps_adam)
+                    fresh[0, s, rows, part] = params - step_dir
+                    fresh[1, s, rows, part] = one_new
+                    fresh[2, s, rows, part] = two_new
                 for a in range(3):
                     give(a, s, i).start()
                 return carry

time: 47.9 us -> 48.2 us (level)
  the two profiles are of different devices: /device:TPU:1 before, /device:TPU:3 now
where the time goes in v8:
time: 48.2 us; the launch traced here: 47.8 us
  Pallas kernels  47.2 us (98%)
  between operations  0.64 us (1%)
    pallas_call x1, Pallas kernels, on_device(): pl.pallas_call(gather_kernel, out_shape=(jax.ShapeDtypeStruct((3, SLOTS,...  41.8 us
    pallas_call x1, Pallas kernels, on_device(): pl.pallas_call(functools.partial(update_kernel, limit), out_shape=[jax.Sh...  5.35 us

profile of v8, /device:TPU:3, one launch (start us, length us, event | category | flops | bytes accessed | tf_op | source)
XLA Modules:
  0.0 47.8 jit_solution(16755234443112000514)
XLA Ops:
  0.6 41.8 %gather_blocks.1 = (s16[3,3,128,1664]{3,2,1,0:T(8,128)(2,1)}, bf16[5,128,1536]{2,1,0:T(8,128)(2,1)}, f32[8,128]{1,0:T(8,128)}, s32[8]{0:T(128)}) custom-call(s32[8]{0:T(128)} %lost_hbm.1, s32[28]{0:T(128)} %blocks_hbm.1, f32[128,1536]{1,0:T(8,128)} %bitcast.7, f32[128,1536]{1,0:T(8,128)} %bitcast.8, f32[128,1536]{1,0:T(8,128)} %bitcast.9, ...), custom_call_target="tpu_custom_call" | custom-call | tf_op jit(solution)/shard_map/gather_blocks/pallas_call | solution.py:394
  42.5 5.3 %adam_update.1 = (f32[384,1536]{1,0:T(8,128)}, f32[384,1536]{1,0:T(8,128)}, f32[384,1536]{1,0:T(8,128)}) custom-call(s32[8]{0:T(128)} %get-tuple-element.10.meta_ref, f32[8,128]{1,0:T(8,128)} %get-tuple-element.11.norm_ref, s16[3,3,128,1664]{3,2,1,0:T(8,128)(2,1)} %get-tuple-element.12.gat_ref, bf16[5,128,1536]{2,1,0:T(8,128)(2,1)} %get-tuple-element.13.gwin_ref), custom_call_target="tpu_custom_call" | custom-call | tf_op jit(solution)/shard_map/adam_update/pallas_call | solution.py:425
